TPU v7x, 512 devices: a whole 4x4x16 slice. The times are simulated.
512 devices in a mesh: dp: 64 (over x, z), tensor: 8 (over y, core).
Axes of the slice: x: 4, y: 4, z: 16, core: 2. Of those that a mesh axis runs over, the one named last changes fastest.
Arguments:
- tiles: bfloat16 [1024, 24, 1280], P('dp', 'tensor'), may hold values from -6 to 6
- window_ids: int32 [1024, 24], P('dp', 'tensor'), may hold values from 0 to 3, never falling along the last dimension, each value on 1 to 12 neighbouring positions
- counts: int32 [64], replicated, may hold values from 0 to 16, as said below
- ln_gain: bfloat16 [1280], replicated, may hold values from 0.099609375 to 1.8984375
- ln_bias: bfloat16 [1280], replicated, may hold values from -3 to 3
- qkv_weight: bfloat16 [3, 1280, 1280], P(None, None, 'tensor'), may hold values from -0.15625 to 0.15625
- qkv_bias: bfloat16 [3, 1280], P(None, 'tensor'), may hold values from -3 to 3
- proj_weight: bfloat16 [1280, 1280], P('tensor'), may hold values from -0.15625 to 0.15625
- proj_bias: bfloat16 [1280], replicated, may hold values from -3 to 3
- mlp_gain: bfloat16 [1280], replicated, may hold values from 0.099609375 to 1.8984375
- mlp_bias: bfloat16 [1280], replicated, may hold values from -3 to 3
- fc1_weight: bfloat16 [1280, 2560], P(None, 'tensor'), may hold values from -0.15625 to 0.15625
- fc1_bias: bfloat16 [2560], P('tensor'), may hold values from -3 to 3
- fc2_weight: bfloat16 [2560, 1280], P('tensor'), may hold values from -0.125 to 0.125
- fc2_bias: bfloat16 [1280], replicated, may hold values from -3 to 3
Outputs:
- encoded: bfloat16 [1024, 24, 1280], P('dp', 'tensor')
Inputs may be any that keep to these rules, and one draw needn't show every extreme that they name: `counts`: for each device d below 32, exactly one of devices d and d + 32 owns tiles, and it owns more than 8; device 0 owns 16, and device 64 / 2 - 1 owns tiles.
All inputs are finite; a program needn't handle non-finite values.
Results may differ from a plain program's by a relative error of at most 0.02.
Values may be sent and summed in bfloat16 or wider, within the bound.
A program may use at most 64 MiB of HBM per device.

v0:
```python
import jax
import jax.numpy as jnp
from jax import lax
from jax.sharding import PartitionSpec as P

HEAD_DIM = 80
PROC = 8


def normalize(tile_rows, gain, shift):
    widened = tile_rows.astype(jnp.float32)
    row_mean = jnp.mean(widened, axis=-1, keepdims=True)
    centred = widened - row_mean
    variance = jnp.mean(centred * centred, axis=-1, keepdims=True)
    normed = centred * lax.rsqrt(variance + 1e-06) * gain.astype(jnp.float32) + shift.astype(
        jnp.float32
    )
    return normed.astype(jnp.bfloat16)


def on_device(
    tiles,
    window_ids,
    counts,
    ln_gain,
    ln_bias,
    qkv_weight,
    qkv_bias,
    proj_weight,
    proj_bias,
    mlp_gain,
    mlp_bias,
    fc1_weight,
    fc1_bias,
    fc2_weight,
    fc2_bias,
):
    peer_count = lax.axis_size("dp")
    half_peers = peer_count // 2
    per_peer = (PROC + 1) // 2
    row_share = tiles.shape[1]
    own_rows = tiles[:PROC]
    spill_rows = tiles[PROC:]
    labels = window_ids.astype(jnp.bfloat16)
    own_labels = labels[:PROC]
    spill_labels = labels[PROC:]
    my_index = lax.axis_index("dp")
    own_count = lax.dynamic_index_in_dim(counts, my_index, 0, keepdims=False)
    device_ids = jnp.arange(peer_count, dtype=jnp.int32)
    partner = (my_index + half_peers) % peer_count
    left_peer = (my_index + peer_count - 1) % peer_count
    left_partner = (left_peer + half_peers) % peer_count
    left_count = jnp.sum(jnp.where(device_ids == left_peer, counts, 0))
    beside = jnp.where(left_count == 0, left_peer, left_partner)
    offsets = jnp.arange(PROC, dtype=jnp.int32)
    target_of = jnp.where(offsets % 2 == 0, partner, beside)
    lent = offsets < own_count - PROC
    move_device = jnp.where(lent, target_of, -1)
    move_slot = jnp.where(lent, offsets, -1)
    target = (move_device[:, None] == device_ids[None, :]).astype(jnp.float32)
    before = jnp.cumsum(target, axis=0) - target
    rank_in_peer = jnp.sum(before * target, axis=1)
    chosen = (
        rank_in_peer[None, None, :] == jnp.arange(per_peer, dtype=jnp.float32)[None, :, None]
    ).astype(jnp.float32)
    picker = jnp.transpose(target)[:, None, :] * chosen
    pick_half = picker.astype(jnp.bfloat16)
    send_rows = jnp.einsum(
        "pko,orf->pkrf", pick_half, spill_rows, preferred_element_type=jnp.float32
    ).astype(jnp.bfloat16)
    send_labels = jnp.einsum(
        "pko,or->pkr", pick_half, spill_labels, preferred_element_type=jnp.float32
    ).astype(jnp.bfloat16)
    send_slot = (jnp.einsum("pko,o->pk", picker, (move_slot + 1).astype(jnp.float32)) - 1.0).astype(
        jnp.bfloat16
    )
    got_rows, got_labels, got_slot = (
        lax.all_to_all(send_rows, "dp", split_axis=0, concat_axis=0, tiled=True),
        lax.all_to_all(send_labels, "dp", split_axis=0, concat_axis=0, tiled=True),
        lax.all_to_all(send_slot, "dp", split_axis=0, concat_axis=0, tiled=True),
    )
    placer = (
        got_slot.astype(jnp.int32)[None, :, :] == jnp.arange(PROC, dtype=jnp.int32)[:, None, None]
    ).astype(jnp.float32)
    filled = jnp.sum(placer, axis=(1, 2)) > 0.5
    place_half = placer.astype(jnp.bfloat16)
    arrived = jnp.einsum(
        "spk,pkrf->srf", place_half, got_rows, preferred_element_type=jnp.float32
    ).astype(jnp.bfloat16)
    arrived_labels = jnp.einsum(
        "spk,pkr->sr", place_half, got_labels, preferred_element_type=jnp.float32
    ).astype(jnp.bfloat16)
    work_rows = jnp.where(filled[:, None, None], arrived, own_rows)
    work_labels = jnp.where(filled[:, None], arrived_labels, own_labels)
    full_rows, full_labels = (
        lax.all_gather(work_rows, "tensor", axis=1, tiled=True),
        lax.all_gather(work_labels, "tensor", axis=1, tiled=True),
    )
    tile_count = full_rows.shape[0]
    tile_len = full_rows.shape[1]
    local_width = qkv_weight.shape[2]
    local_heads = local_width // HEAD_DIM
    normed = normalize(full_rows, ln_gain, ln_bias).reshape(
        tile_count * tile_len, full_rows.shape[2]
    )

    def project_heads(which):
        values_out = jnp.dot(
            normed, qkv_weight[which], preferred_element_type=jnp.float32
        ) + qkv_bias[which].astype(jnp.float32)
        return values_out.astype(jnp.bfloat16).reshape(tile_count, tile_len, local_heads, HEAD_DIM)

    query = project_heads(0)
    keys = project_heads(1)
    values = project_heads(2)
    scores = jnp.einsum(
        "ntha,nsha->nhts", query, keys, preferred_element_type=jnp.float32
    ) / jnp.sqrt(jnp.float32(HEAD_DIM))
    same_window = full_labels[:, None, :, None] == full_labels[:, None, None, :]
    weights = jnp.where(same_window, jnp.exp(scores), jnp.float32(0.0))
    attention = (weights / jnp.sum(weights, axis=-1, keepdims=True)).astype(jnp.bfloat16)
    attended = jnp.einsum(
        "nhts,nsha->ntha", attention, values, preferred_element_type=jnp.float32
    ).astype(jnp.bfloat16)
    columns = jnp.swapaxes(attended.reshape(tile_count, tile_len, local_width), 0, 1)
    piece = columns
    summed_all = lax.psum(
        jnp.einsum("tnc,cf->tnf", piece, proj_weight, preferred_element_type=jnp.float32).astype(
            jnp.bfloat16
        ),
        "tensor",
    ).astype(jnp.float32)
    mixed_full = (
        summed_all
        + proj_bias.astype(jnp.float32)
        + jnp.swapaxes(full_rows, 0, 1).astype(jnp.float32)
    ).astype(jnp.bfloat16)
    my_mixed = lax.dynamic_slice_in_dim(
        mixed_full, lax.axis_index("tensor") * row_share, row_share, 0
    )
    normed2 = normalize(mixed_full, mlp_gain, mlp_bias)
    lifted = jnp.einsum(
        "tnf,fh->tnh", normed2, fc1_weight, preferred_element_type=jnp.float32
    ) + fc1_bias.astype(jnp.float32)
    hidden = (lifted * jax.nn.sigmoid(1.702 * lifted)).astype(jnp.bfloat16)
    piece = hidden
    ffn_share = lax.psum_scatter(
        jnp.einsum("tnh,hf->tnf", piece, fc2_weight, preferred_element_type=jnp.float32).astype(
            jnp.bfloat16
        ),
        "tensor",
        scatter_dimension=0,
        tiled=True,
    ).astype(jnp.float32)
    out_rows = ffn_share + fc2_bias.astype(jnp.float32) + my_mixed.astype(jnp.float32)
    mixed_rows = jnp.swapaxes(out_rows.astype(jnp.bfloat16), 0, 1)
    back_rows = jnp.einsum(
        "spk,srf->pkrf", place_half, mixed_rows, preferred_element_type=jnp.float32
    ).astype(jnp.bfloat16)
    returned = lax.all_to_all(back_rows, "dp", split_axis=0, concat_axis=0, tiled=True)
    spill_out = jnp.einsum(
        "pko,pkrf->orf", pick_half, returned, preferred_element_type=jnp.float32
    ).astype(jnp.bfloat16)
    slot_index = jnp.arange(2 * PROC, dtype=jnp.int32)
    live_slots = slot_index < own_count
    result = jnp.concatenate([mixed_rows, spill_out], axis=0)
    return jnp.where(live_slots[:, None, None], result, jnp.zeros_like(result))


def solution(mesh):
    placed = (
        P("dp", "tensor", None),
        P("dp", "tensor"),
        P(),
        P(),
        P(),
        P(None, None, "tensor"),
        P(None, "tensor"),
        P("tensor", None),
        P(),
        P(),
        P(),
        P(None, "tensor"),
        P("tensor"),
        P("tensor", None),
        P(),
    )
    return jax.shard_map(
        on_device, mesh=mesh, in_specs=placed, out_specs=P("dp", "tensor", None), check_vma=False
    )
```

profile of v0, /device:TPU:1, one launch (start us, length us, event | category | flops | bytes accessed | tf_op | source)
XLA Modules:
  0.0 404.4 jit_solution(12437028099563145654)
XLA Ops:
  6.5 1.4 fusion.93
  8.6 1.3 dynamic_slice.7
  11.8 19.1 %all-to-all-start = ((bf16[64,1,4]{2,1,0:T(2,128)(2,1)}), bf16[64,1,4]{2,1,0:T(2,128)(2,1)S(1)}, u32[]{:S(2)}, u32[]{:S(2)}) async-start(bf16[64,1,4]{2,1,0:T(2,128)(2,1)} %copy.73), calls=%async_computation | async-start | bytes 65536 | tf_op jit(solution)/shard_map/all_to_all | solution.py:80
  32.6 11.7 %all-to-all-done = bf16[64,1,4]{2,1,0:T(2,128)(2,1)S(1)} async-done(((bf16[64,1,4]{2,1,0:T(2,128)(2,1)}), bf16[64,1,4]{2,1,0:T(2,128)(2,1)S(1)}, u32[]{:S(2)}, u32[]{:S(2)}) %all-to-all-start) | async-done | bytes 544 | tf_op jit(solution)/shard_map/all_to_all | solution.py:80
  44.3 4.6 %all-to-all-start.2 = ((bf16[64,4,3]{2,1,0:T(4,128)(2,1)}), bf16[64,4,3]{2,1,0:T(4,128)(2,1)S(1)}, u32[]{:S(2)}, u32[]{:S(2)}) async-start(bf16[64,4,3]{2,1,0:T(4,128)(2,1)} %copy.79), calls=%async_computation.2 | async-start | bytes 131072 | tf_op jit(solution)/shard_map/all_to_all | solution.py:79
  48.9 1.6 convolution_convert_fusion.1
  50.5 2.8 copy.75
  53.3 9.1 %all-to-all-done.2 = bf16[64,4,3]{2,1,0:T(4,128)(2,1)S(1)} async-done(((bf16[64,4,3]{2,1,0:T(4,128)(2,1)}), bf16[64,4,3]{2,1,0:T(4,128)(2,1)S(1)}, u32[]{:S(2)}, u32[]{:S(2)}) %all-to-all-start.2) | async-done | bytes 1568 | tf_op jit(solution)/shard_map/all_to_all | solution.py:79
  62.4 5.6 %all-to-all-start.1 = ((bf16[64,4,3,1280]{3,1,2,0:T(4,128)(2,1)}), bf16[64,4,3,1280]{3,1,2,0:T(4,128)(2,1)S(1)}, u32[]{:S(2)}, u32[]{:S(2)}) async-start(bf16[64,4,3,1280]{3,1,2,0:T(4,128)(2,1)} %copy.75), calls=%async_computation.1 | async-start | bytes 3932160 | tf_op jit(solution)/shard_map/all_to_all | solution.py:78
  68.6 13.1 %all-gather = bf16[8,3,8]{2,1,0:T(4,128)(2,1)S(1)} all-gather(bf16[1,3,8]{2,1,0:T(4,128)(2,1)S(1)} %fusion.17), channel_id=1, replica_groups=mesh['dp'=64,'tensor'=8] {'tensor'}, dimensions={0}, use_global_device_ids=true | all-gather | bytes 432 | tf_op jit(solution)/shard_map/all_gather | solution.py:97
  81.9 72.5 %all-to-all-done.1 = bf16[64,4,3,1280]{3,1,2,0:T(4,128)(2,1)S(1)} async-done(((bf16[64,4,3,1280]{3,1,2,0:T(4,128)(2,1)}), bf16[64,4,3,1280]{3,1,2,0:T(4,128)(2,1)S(1)}, u32[]{:S(2)}, u32[]{:S(2)}) %all-to-all-start.1) | async-done | bytes 1966112 | tf_op jit(solution)/shard_map/all_to_all | solution.py:78
  154.8 20.8 %all_gather.6 = bf16[8,24,1280]{2,0,1:T(8,128)(2,1)S(1)} all-gather(bf16[8,3,1280]{2,0,1:T(8,128)(2,1)S(1)} %fusion.2), channel_id=1, replica_groups=mesh['dp'=64,'tensor'=8] {'tensor'}, dimensions={1}, use_global_device_ids=true | all-gather | bytes 552960 | tf_op jit(solution)/shard_map/all_gather | solution.py:96
  176.6 1.3 fusion.12
  178.1 1.3 fusion.13
  179.6 1.3 fusion.11
  181.9 1.1 convolution_convert_fusion.3
  183.3 66.3 %all-reduce.2.cloned.1.call-done = bf16[24,8,1280]{2,1,0:T(8,128)(2,1)} async-done(((bf16[24,8,1280]{2,1,0:T(8,128)(2,1)}), bf16[24,8,1280]{2,1,0:T(8,128)(2,1)}) %all-reduce.2.cloned.1.call-update) | async-done | bytes 491536 | tf_op jit(solution)/shard_map/psum | solution.py:127
  249.7 1.3 convert_reduce_fusion.1
  251.3 2.9 convolution_convert_fusion.2
  254.2 37.6 %reduce-scatter.2.cloned.1.call-done = bf16[3,8,1280]{2,1,0:T(8,128)(2,1)} async-done(((bf16[24,8,1280]{2,1,0:T(8,128)(2,1)}), bf16[3,8,1280]{2,1,0:T(8,128)(2,1)}) %reduce-scatter.2.cloned.1.call-update) | async-done | bytes 61456 | tf_op jit(solution)/shard_map/reduce_scatter | solution.py:147
  291.8 1.5 convolution_convert_fusion
  293.3 2.8 copy.91
  296.1 14.4 %all-to-all-start.3 = ((bf16[64,4,3,1280]{3,1,2,0:T(4,128)(2,1)}), bf16[64,4,3,1280]{3,1,2,0:T(4,128)(2,1)S(1)}, u32[]{:S(2)}, u32[]{:S(2)}) async-start(bf16[64,4,3,1280]{3,1,2,0:T(4,128)(2,1)} %copy.91), calls=%async_computation.4 | async-start | bytes 3932160 | tf_op jit(solution)/shard_map/all_to_all | solution.py:160
  311.2 85.1 %all-to-all-done.3 = bf16[64,4,3,1280]{3,1,2,0:T(4,128)(2,1)S(1)} async-done(((bf16[64,4,3,1280]{3,1,2,0:T(4,128)(2,1)}), bf16[64,4,3,1280]{3,1,2,0:T(4,128)(2,1)S(1)}, u32[]{:S(2)}, u32[]{:S(2)}) %all-to-all-start.3) | async-done | bytes 1966112 | tf_op jit(solution)/shard_map/all_to_all | solution.py:160
  (80 shorter events, 8.7 us)
Async XLA Ops:
  6.5 244.7 %copy-start = (bf16[320,1280]{1,0:T(8,128)(2,1)S(1)}, bf16[320,1280]{1,0:T(8,128)(2,1)}, u32[]{:S(2)}) copy-start(bf16[320,1280]{1,0:T(8,128)(2,1)} %param.28) | copy-start | bytes 2457604
  11.8 32.4 %all-to-all-start = ((bf16[64,1,4]{2,1,0:T(2,128)(2,1)}), bf16[64,1,4]{2,1,0:T(2,128)(2,1)S(1)}, u32[]{:S(2)}, u32[]{:S(2)}) async-start(bf16[64,1,4]{2,1,0:T(2,128)(2,1)} %copy.73), calls=%async_computation | async-start | bytes 65536 | tf_op jit(solution)/shard_map/all_to_all | solution.py:80
  44.3 18.1 %all-to-all-start.2 = ((bf16[64,4,3]{2,1,0:T(4,128)(2,1)}), bf16[64,4,3]{2,1,0:T(4,128)(2,1)S(1)}, u32[]{:S(2)}, u32[]{:S(2)}) async-start(bf16[64,4,3]{2,1,0:T(4,128)(2,1)} %copy.79), calls=%async_computation.2 | async-start | bytes 131072 | tf_op jit(solution)/shard_map/all_to_all | solution.py:79
  53.3 14.8 %copy-start.5 = (bf16[1280]{0:T(1024)(128)(2,1)S(1)}, bf16[1280]{0:T(1024)(128)(2,1)}, u32[]{:S(2)}) copy-start(bf16[1280]{0:T(1024)(128)(2,1)} %param.18) | copy-start | bytes 7684
  53.3 14.8 %copy-start.6 = (bf16[1280]{0:T(1024)(128)(2,1)S(1)}, bf16[1280]{0:T(1024)(128)(2,1)}, u32[]{:S(2)}) copy-start(bf16[1280]{0:T(1024)(128)(2,1)} %param.19) | copy-start | bytes 7684
  53.3 14.8 %copy-start.4 = (bf16[3,160]{1,0:T(4,128)(2,1)S(1)}, bf16[3,160]{1,0:T(4,128)(2,1)}, u32[]{:S(2)}) copy-start(bf16[3,160]{1,0:T(4,128)(2,1)} %param.21) | copy-start | bytes 2884
  53.3 101.1 %copy-start.3 = (bf16[16,3,1280]{2,0,1:T(8,128)(2,1)S(1)}, bf16[16,3,1280]{2,0,1:T(8,128)(2,1)}, u32[]{:S(2)}) copy-start(bf16[16,3,1280]{2,0,1:T(8,128)(2,1)} %param.15) | copy-start | bytes 368644
  62.4 92.0 %all-to-all-start.1 = ((bf16[64,4,3,1280]{3,1,2,0:T(4,128)(2,1)}), bf16[64,4,3,1280]{3,1,2,0:T(4,128)(2,1)S(1)}, u32[]{:S(2)}, u32[]{:S(2)}) async-start(bf16[64,4,3,1280]{3,1,2,0:T(4,128)(2,1)} %copy.75), calls=%async_computation.1 | async-start | bytes 3932160 | tf_op jit(solution)/shard_map/all_to_all | solution.py:78
  68.0 181.6 %all-reduce.2.cloned.1.call-start = ((), (), s32[]{:S(2)}) async-start(), calls=%async_computation.5 | async-start | bytes 983040 | tf_op jit(solution)/shard_map/psum | solution.py:127
  179.4 2.5 copy-start.1
  181.0 2.3 copy-start.7
  181.0 2.3 copy-start.8
  181.0 2.3 copy-start.9
  181.0 2.3 copy-start.11
  183.0 108.7 %reduce-scatter.2.cloned.1.call-start = ((), (), s32[]{:S(2)}) async-start(), calls=%async_computation.6 | async-start | bytes 552960 | tf_op jit(solution)/shard_map/reduce_scatter | solution.py:147
  251.3 2.9 copy-start.10
  296.1 15.1 %copy-start.2 = (bf16[3,8,1280]{2,1,0:T(8,128)(2,1)S(1)}, bf16[3,8,1280]{2,1,0:T(8,128)(2,1)}, u32[]{:S(2)}) copy-start(bf16[3,8,1280]{2,1,0:T(8,128)(2,1)} %reduce-scatter.2.cloned.1.call-done) | copy-start | bytes 184324
  296.1 100.2 %all-to-all-start.3 = ((bf16[64,4,3,1280]{3,1,2,0:T(4,128)(2,1)}), bf16[64,4,3,1280]{3,1,2,0:T(4,128)(2,1)S(1)}, u32[]{:S(2)}, u32[]{:S(2)}) async-start(bf16[64,4,3,1280]{3,1,2,0:T(4,128)(2,1)} %copy.91), calls=%async_computation.4 | async-start | bytes 3932160 | tf_op jit(solution)/shard_map/all_to_all | solution.py:160
Sparse Core Ops, SparseCore 0:
  183.1 66.4 all-reduce.1
  254.3 37.4 reduce-scatter.1
where the time goes:
time: 412 us; the launch traced here: 404 us
  waiting for transfers between devices  282 us (68%)
  starting transfers between devices  44 us (11%)
  blocking collectives  33.9 us (8%)
  between operations  15.2 us (4%)
  matrix products  13 us (3%)
  local copies, waits for them, and re-layouts  9.51 us (2%)
  other arithmetic  6.57 us (2%)
    all_to_all x1, waiting for transfers between devices, on_device(): lax.all_to_all(back_rows, 'dp', split_axis=0, concat_axis=0, tiled=True)  85.1 us
    all_to_all x1, waiting for transfers between devices, on_device(): lax.all_to_all(send_rows, 'dp', split_axis=0, concat_axis=0, tiled=True)  72.5 us
    psum x1, waiting for transfers between devices, on_device(): lax.psum(jnp.einsum('tnc,cf->tnf', piece, proj_weight, preferred_element_...  66.3 us
    reduce_scatter x1, waiting for transfers between devices, on_device(): lax.psum_scatter(jnp.einsum('tnh,hf->tnf', piece, fc2_weight, preferred_e...  37.6 us
    all_gather x1, blocking collectives, on_device(): lax.all_gather(work_rows, 'tensor', axis=1, tiled=True)  20.8 us
    all_to_all x1, starting transfers between devices, on_device(): lax.all_to_all(send_slot, 'dp', split_axis=0, concat_axis=0, tiled=True)  19.1 us
    all_to_all x1, starting transfers between devices, on_device(): lax.all_to_all(back_rows, 'dp', split_axis=0, concat_axis=0, tiled=True)  14.4 us
    all_gather x1, blocking collectives, on_device(): lax.all_gather(work_labels, 'tensor', axis=1, tiled=True)  13.1 us
  transfers between devices with their start and end apart: 6, of which 6 were waited for; matrix products, arithmetic and copies ran while one was open for 2% of the time, Pallas kernels for 0%

commit v1 on v0

v1 whole, which is shorter than its diff:
```python
import jax
import jax.numpy as jnp
from jax import lax
from jax.experimental import pallas as pl
from jax.experimental.pallas import tpu as pltpu
from jax.sharding import PartitionSpec as P

D = 1280
HEAD_DIM = 80
LANES = 128
WIDE = D + LANES
QUARTER = 16
ROWS = 24
CHIPS = 4
GROUP = CHIPS * ROWS
MESH = pl.DeviceIdType.MESH
F32 = jnp.float32
BF16 = jnp.bfloat16


def matmul(left, right):
    return jnp.dot(left, right, preferred_element_type=F32)


def matmul_t(left, right):
    return lax.dot_general(left, right, (((1,), (1,)), ((), ())), preferred_element_type=F32)


def normalize(rows, gain, shift):
    centred = rows - jnp.mean(rows, axis=-1, keepdims=True)
    variance = jnp.mean(centred * centred, axis=-1, keepdims=True)
    return (centred * lax.rsqrt(variance + 1e-06) * gain + shift).astype(BF16)


def iotas(shape):
    return (
        lax.broadcasted_iota(jnp.int32, shape, 0),
        lax.broadcasted_iota(jnp.int32, shape, 1),
    )


def one_hot(flags):
    return jnp.where(flags, 1.0, 0.0).astype(BF16)


def encode(
    counts,
    window,
    vectors,
    tiles,
    qkv_weight,
    proj_weight,
    fc1_weight,
    fc2_weight,
    out,
    vec,
    wqkv,
    wproj,
    wfc1,
    wfc2,
    tile_rows,
    quarter_out,
    quarter_in,
    normed_all,
    part_out,
    part_in,
    normed2_all,
    ffn_out,
    ffn_in,
    done_out,
    done_in,
    load_sem,
    weight_send,
    weight_recv,
    lend_send,
    lend_recv,
    ring_send,
    ring_recv,
    back_send,
    back_recv,
):
    d, t = lax.axis_index("dp"), lax.axis_index("tensor")
    y, c = t // 2, t % 2
    pd = (d + 32) % 64
    sib = y * 2 + (1 - c)
    around = [(d, ((y + k) % CHIPS) * 2 + c) for k in (2, 1, 3)]
    beside = [(d, sib), (pd, t), (pd, sib)]

    barrier = pltpu.get_barrier_semaphore()
    for peer in beside + around:
        pl.semaphore_signal(barrier, inc=1, device_id=peer, device_id_type=MESH)

    loads = [(tiles, tile_rows), (vectors, vec.at[c])]
    pushes = [(vectors, vec.at[c])]
    for which in range(3):
        for head in range(2):
            pair = (
                qkv_weight.at[which, pl.ds(head * HEAD_DIM, HEAD_DIM)],
                wqkv.at[c, which, head, pl.ds(0, HEAD_DIM)],
            )
            loads.append(pair)
            pushes.append(pair)
    for head in range(2):
        pair = (
            proj_weight.at[pl.ds(head * HEAD_DIM, HEAD_DIM)],
            wproj.at[c, head, pl.ds(0, HEAD_DIM)],
        )
        loads.append(pair)
        pushes.append(pair)
    for pair in ((fc1_weight, wfc1.at[c]), (fc2_weight, wfc2.at[c])):
        loads.append(pair)
        pushes.append(pair)
    started = []
    for i, (src, dst) in enumerate(loads):
        started.append(pltpu.make_async_copy(src, dst, load_sem.at[i]))
        started[-1].start()

    gap = jnp.zeros((LANES - HEAD_DIM, D), BF16)
    for core in range(2):
        for head in range(2):
            for which in range(3):
                wqkv[core, which, head, HEAD_DIM:] = gap
            wproj[core, head, HEAD_DIM:] = gap

    own_count = counts[d]
    pair_count = own_count + counts[pd]
    side = jnp.where(own_count > 0, 0, 1)

    row, col = iotas((16, 16))
    labels = []
    for token in range(3):
        picked = jnp.where(row == col, window[token : token + 1, :].astype(F32), 0.0)
        labels.append(jnp.sum(picked, axis=1, keepdims=True))
    labels = jnp.broadcast_to(jnp.concatenate(labels, axis=0), (48, LANES)).astype(BF16)
    row, col = iotas((64, 48))
    inner = row % QUARTER
    pick = one_hot((inner < 12) & (col == (inner // 4) * 16 + (row // QUARTER) * 4 + inner % 4))
    started[0].wait()
    features = tile_rows[...].reshape(48, D)
    quarters = matmul(pick, jnp.concatenate([features, labels], axis=1))
    quarter_out[...] = quarters.astype(BF16).reshape(4, QUARTER, WIDE)
    quarter_in[0, c] = quarter_out[c]

    pl.semaphore_wait(barrier, len(beside) + len(around))

    def remote(src, dst, sems, peer):
        copy = pltpu.make_async_remote_copy(
            src_ref=src,
            dst_ref=dst,
            send_sem=sems[0],
            recv_sem=sems[1],
            device_id=peer,
            device_id_type=MESH,
        )
        copy.start()
        return copy

    sent = []
    lends = []
    for i, (peer, block, where) in enumerate(
        (
            (beside[1], 2 + c, 1),
            (beside[2], 3 - c, 1),
            (beside[0], 1 - c, 0),
        )
    ):
        lends.append(
            remote(
                quarter_out.at[block],
                quarter_in.at[where, c],
                (lend_send.at[i], lend_recv.at[i]),
                peer,
            )
        )
    pushed = []
    for i, (src, dst) in enumerate(pushes):
        pushed.append(remote(src, dst, (weight_send.at[i], weight_recv.at[i]), beside[0]))
    sent += lends + pushed
    for copy in lends:
        copy.wait_recv()

    row, col = iotas((ROWS, 64))
    inner = col % QUARTER
    pick = one_hot(
        (inner < 12) & (col // 32 == side) & (row == ((col % 32) // QUARTER) * 12 + inner)
    )
    mine = matmul(pick, quarter_in[...].reshape(64, WIDE))
    rows_in = mine[:, :D]

    started[1].wait()

    def vector(i):
        return vec[c, i : i + 1, :].astype(F32)

    def spread(buffer, phase):
        copies = []
        for i, peer in enumerate(around):
            copies.append(
                remote(
                    buffer.at[y],
                    buffer.at[y],
                    (ring_send.at[phase, i], ring_recv.at[phase, i]),
                    peer,
                )
            )
        return copies

    def scatter(source, target, phase):
        copies = []
        for i, peer in enumerate(around):
            copies.append(
                remote(
                    source.at[peer[1] // 2],
                    target.at[y],
                    (ring_send.at[phase, i], ring_recv.at[phase, i]),
                    peer,
                )
            )
        return copies

    def arrive(copies):
        for copy in copies:
            copy.wait_recv()
        sent.extend(copies)

    def gathered(buffer):
        return jnp.concatenate(
            [buffer[i].astype(F32) for i in range(CHIPS)], axis=0
        ).astype(BF16)

    def total(buffer):
        out_sum = buffer[0].astype(F32)
        for i in range(1, CHIPS):
            out_sum = out_sum + buffer[i].astype(F32)
        return out_sum

    normed = normalize(rows_in, vector(0), vector(1))
    normed_all[y] = jnp.concatenate([normed, mine[:, D:].astype(BF16)], axis=1)
    copies = spread(normed_all, 0)

    for copy in started[2:]:
        copy.wait()
    for copy in pushed[:7]:
        copy.wait_recv()
    arrive(copies)

    everything = gathered(normed_all)
    row, lane = iotas((GROUP, LANES))
    key = everything[:, D:].astype(F32).astype(jnp.int32) + 4 * (row % 4)
    marks = one_hot(lane == key)
    same = matmul_t(marks, marks) > 0.5
    width = 6 * LANES
    qkv_bias = jnp.concatenate(
        [vec[core, 6:7, :width].astype(F32) for core in range(2)], axis=1
    )
    qkv = matmul_t(everything[:, :D], wqkv[...].reshape(2 * width, D)) + qkv_bias
    qkv = qkv.astype(BF16)
    scale = 1.0 / (float(HEAD_DIM) ** 0.5)
    attended = []
    for core in range(2):
        for head in range(2):
            base = core * width + head * LANES
            query = qkv[:, base : base + LANES]
            keys = qkv[:, base + 2 * LANES : base + 3 * LANES]
            values = qkv[:, base + 4 * LANES : base + 5 * LANES]
            scores = matmul_t(query, keys) * scale
            weights = jnp.where(same, jnp.exp(scores), 0.0)
            weights = weights / jnp.sum(weights, axis=1, keepdims=True)
            attended.append(matmul(weights.astype(BF16), values).astype(BF16))
    attended = jnp.concatenate(attended, axis=1)
    for copy in pushed[7:9]:
        copy.wait_recv()
    mixed_part = matmul(attended, wproj[...].reshape(4 * LANES, D))
    part_out[...] = mixed_part.reshape(CHIPS, ROWS, D).astype(BF16)
    part_in[y] = part_out[y]
    arrive(scatter(part_out, part_in, 1))

    mixed = (total(part_in) + vector(2) + rows_in).astype(BF16).astype(F32)
    normed2_all[y] = normalize(mixed, vector(3), vector(4))
    copies = spread(normed2_all, 2)
    for copy in pushed[9:]:
        copy.wait_recv()
    arrive(copies)

    fc1_bias = jnp.concatenate([vec[core, 7:8, :320].astype(F32) for core in range(2)], axis=1)
    lifted = matmul_t(gathered(normed2_all), wfc1[...].reshape(640, D)) + fc1_bias
    hidden = (lifted * jax.nn.sigmoid(1.702 * lifted)).astype(BF16)
    ffn_part = matmul(hidden, wfc2[...].reshape(640, D))
    ffn_out[...] = ffn_part.reshape(CHIPS, ROWS, D).astype(BF16)
    ffn_in[y] = ffn_out[y]
    arrive(scatter(ffn_out, ffn_in, 3))

    row, col = iotas((ROWS, D))
    slot = 4 * (2 * side + c) + row % 4
    encoded = jnp.where(slot < pair_count, total(ffn_in) + vector(5) + mixed, 0.0).astype(BF16)
    row, col = iotas((32, ROWS))
    inner = row % QUARTER
    pick = one_hot((inner < 12) & (col == (row // QUARTER) * 12 + inner))
    done_out[...] = matmul(pick, encoded).astype(BF16).reshape(2, QUARTER, D)
    done_in[0, c] = done_out[c]
    backs = []
    for i, (peer, block, where) in enumerate(
        ((beside[1], c, 1), (beside[2], 1 - c, 1), (beside[0], 1 - c, 0))
    ):
        backs.append(
            remote(
                done_out.at[block],
                done_in.at[where, c],
                (back_send.at[i], back_recv.at[i]),
                peer,
            )
        )
    arrive(backs)

    row, col = iotas((48, 64))
    inner = col % QUARTER
    pick = one_hot(
        (inner < 12)
        & (row == (inner // 4) * 16 + (col // QUARTER) * 4 + inner % 4)
        & (side == 0)
    )
    out[...] = matmul(pick, done_in[...].reshape(64, D)).astype(BF16).reshape(3, 16, D)
    for copy in sent:
        copy.wait_send()


def on_device(
    tiles,
    window_ids,
    counts,
    ln_gain,
    ln_bias,
    qkv_weight,
    qkv_bias,
    proj_weight,
    proj_bias,
    mlp_gain,
    mlp_bias,
    fc1_weight,
    fc1_bias,
    fc2_weight,
    fc2_bias,
):
    heads_bias = jnp.pad(qkv_bias.reshape(6, HEAD_DIM), ((0, 0), (0, LANES - HEAD_DIM)))
    vectors = jnp.stack(
        [
            ln_gain,
            ln_bias,
            proj_bias,
            mlp_gain,
            mlp_bias,
            fc2_bias,
            jnp.pad(heads_bias.reshape(768), (0, D - 768)),
            jnp.pad(fc1_bias, (0, D - 320)),
        ]
        + [jnp.zeros((D,), BF16)] * 8
    )
    vmem = pl.BlockSpec(memory_space=pltpu.VMEM)
    hbm = pl.BlockSpec(memory_space=pltpu.HBM)
    encoded = pl.pallas_call(
        encode,
        out_shape=jax.ShapeDtypeStruct((3, 16, D), BF16),
        in_specs=[pl.BlockSpec(memory_space=pltpu.SMEM), vmem, hbm, hbm, hbm, hbm, hbm, hbm],
        out_specs=vmem,
        scratch_shapes=[
            pltpu.VMEM((2, 16, D), BF16),
            pltpu.VMEM((2, 3, 2, LANES, D), BF16),
            pltpu.VMEM((2, 2, LANES, D), BF16),
            pltpu.VMEM((2, 320, D), BF16),
            pltpu.VMEM((2, 320, D), BF16),
            pltpu.VMEM((3, 16, D), BF16),
            pltpu.VMEM((4, QUARTER, WIDE), BF16),
            pltpu.VMEM((2, 2, QUARTER, WIDE), BF16),
            pltpu.VMEM((CHIPS, ROWS, WIDE), BF16),
            pltpu.VMEM((CHIPS, ROWS, D), BF16),
            pltpu.VMEM((CHIPS, ROWS, D), BF16),
            pltpu.VMEM((CHIPS, ROWS, D), BF16),
            pltpu.VMEM((CHIPS, ROWS, D), BF16),
            pltpu.VMEM((CHIPS, ROWS, D), BF16),
            pltpu.VMEM((2, QUARTER, D), BF16),
            pltpu.VMEM((2, 2, QUARTER, D), BF16),
            pltpu.SemaphoreType.DMA((12,)),
            pltpu.SemaphoreType.DMA((11,)),
            pltpu.SemaphoreType.DMA((11,)),
            pltpu.SemaphoreType.DMA((3,)),
            pltpu.SemaphoreType.DMA((3,)),
            pltpu.SemaphoreType.DMA((4, 3)),
            pltpu.SemaphoreType.DMA((4, 3)),
            pltpu.SemaphoreType.DMA((3,)),
            pltpu.SemaphoreType.DMA((3,)),
        ],
        compiler_params=pltpu.CompilerParams(
            collective_id=0, has_side_effects=True, vmem_limit_bytes=48 * 2**20
        ),
        name="encode",
    )(
        counts,
        jnp.transpose(window_ids),
        vectors,
        jnp.transpose(tiles, (1, 0, 2)),
        jnp.swapaxes(qkv_weight, 1, 2),
        proj_weight,
        jnp.transpose(fc1_weight),
        fc2_weight,
    )
    return jnp.transpose(encoded, (1, 0, 2))


def solution(mesh):
    placed = (
        P("dp", "tensor", None),
        P("dp", "tensor"),
        P(),
        P(),
        P(),
        P(None, None, "tensor"),
        P(None, "tensor"),
        P("tensor", None),
        P(),
        P(),
        P(),
        P(None, "tensor"),
        P("tensor"),
        P("tensor", None),
        P(),
    )
    return jax.shard_map(
        on_device, mesh=mesh, in_specs=placed, out_specs=P("dp", "tensor", None), check_vma=False
    )
```

time: 412 us -> 55.1 us (0.13); the launches traced: 404 us -> 54.5 us
  waiting for transfers between devices: 282 us -> 0 us
  starting transfers between devices: 44 us -> 0 us
  Pallas kernels: 0 us -> 41.3 us
  blocking collectives: 33.9 us -> 0 us
  between operations: 15.2 us -> 0.03 us
  matrix products: 13 us -> 0 us
  other arithmetic: 6.57 us -> 0 us
    all_to_all x4 -> x0, waiting for transfers between devices: 178 us -> none  [the longest x1 85.1 us: on_device(): lax.all_to_all(back_rows, 'dp', split_axis=0, concat_axis=0, tiled=True)]
    psum x1 -> x0, waiting for transfers between devices: 66.3 us -> none  [on_device(): lax.psum(jnp.einsum('tnc,cf->tnf', piece, proj_weight, preferred_element_...]
    all_to_all x4 -> x0, starting transfers between devices: 43.7 us -> none  [the longest x1 19.1 us: on_device(): lax.all_to_all(send_slot, 'dp', split_axis=0, concat_axis=0, tiled=True)]
    pallas_call x0 -> x1, Pallas kernels: none -> 41.3 us  [on_device(): pl.pallas_call(encode, out_shape=jax.ShapeDtypeStruct((3, 16, D), BF16),...]
    reduce_scatter x1 -> x0, waiting for transfers between devices: 37.6 us -> none  [on_device(): lax.psum_scatter(jnp.einsum('tnh,hf->tnf', piece, fc2_weight, preferred_e...]
    all_gather x2 -> x0, blocking collectives: 33.9 us -> none  [the longest x1 20.8 us: on_device(): lax.all_gather(work_rows, 'tensor', axis=1, tiled=True)]
    dot_general x14 -> x0, matrix products: 13 us -> none  [the longest x3 3.94 us: project_heads(): jnp.dot(normed, qkv_weight[which], preferred_element_type=jnp.float32)]
    unnamed x26 -> x15, local copies, waits for them, and re-layouts: 0.16 us -> 7.46 us
  transfers between devices with their start and end apart: 6 -> 0, of which waited for: 6 -> 0; matrix products, arithmetic and copies ran while one was open for 2% -> 0% of each run, Pallas kernels for 0% -> 0%
where the time goes in v1:
time: 55.1 us; the launch traced here: 54.5 us
  Pallas kernels  41.3 us (75%)
  local copies, waits for them, and re-layouts  13.2 us (24%)
    pallas_call x1, Pallas kernels, on_device(): pl.pallas_call(encode, out_shape=jax.ShapeDtypeStruct((3, 16, D), BF16),...  41.3 us
    unnamed x15, local copies, waits for them, and re-layouts  7.46 us
    another operation x10, local copies, waits for them, and re-layouts, on_device(): jnp.stack([ln_gain, ln_bias, proj_bias, mlp_gain, mlp_bias, fc2_bias, jnp...  4.24 us

profile of v1, /device:TPU:1, one launch (start us, length us, event | category | flops | bytes accessed | tf_op | source)
XLA Modules:
  0.0 54.5 jit_solution(3581958647719744354)
XLA Ops:
  0.0 0.8 %reshape.6 = bf16[6,80]{1,0:T(8,128)(2,1)S(1)} reshape(bf16[3,160]{1,0:T(4,128)(2,1)} %param.21) | data formatting | bytes 1920 | tf_op jit(solution)/shard_map/reshape | solution.py:344
  0.8 0.7 %pad.14 = bf16[1280]{0:T(1024)(128)(2,1)S(1)} pad(bf16[320]{0:T(512)(128)(2,1)} %param.27, bf16[]{:T(256)} %constant.1.clone.1), padding=0_960 | pad | bytes 3202 | tf_op jit(solution)/shard_map/jit(_pad)/pad | solution.py:354
  1.5 0.7 %stack.30 = bf16[1,1280]{1,0:T(2,128)(2,1)S(1)} reshape(bf16[1280]{0:T(1024)(128)(2,1)} %param.18) | data formatting | bytes 5120 | tf_op jit(solution)/shard_map/stack | solution.py:345
  2.2 0.7 %stack.31 = bf16[1,1280]{1,0:T(2,128)(2,1)S(1)} reshape(bf16[1280]{0:T(1024)(128)(2,1)} %param.19) | data formatting | bytes 5120 | tf_op jit(solution)/shard_map/stack | solution.py:345
  2.9 0.7 %stack.32 = bf16[1,1280]{1,0:T(2,128)(2,1)S(1)} reshape(bf16[1280]{0:T(1024)(128)(2,1)} %param.23) | data formatting | bytes 5120 | tf_op jit(solution)/shard_map/stack | solution.py:345
  3.6 0.7 %stack.33 = bf16[1,1280]{1,0:T(2,128)(2,1)S(1)} reshape(bf16[1280]{0:T(1024)(128)(2,1)} %param.24) | data formatting | bytes 5120 | tf_op jit(solution)/shard_map/stack | solution.py:345
  4.3 0.7 %stack.34 = bf16[1,1280]{1,0:T(2,128)(2,1)S(1)} reshape(bf16[1280]{0:T(1024)(128)(2,1)} %param.25) | data formatting | bytes 5120 | tf_op jit(solution)/shard_map/stack | solution.py:345
  4.9 0.7 %stack.35 = bf16[1,1280]{1,0:T(2,128)(2,1)S(1)} reshape(bf16[1280]{0:T(1024)(128)(2,1)} %param.29) | data formatting | bytes 5120 | tf_op jit(solution)/shard_map/stack | solution.py:345
  5.6 0.1 stack.39.vectors
  5.7 0.0 copy-start
  5.7 1.3 %copy-done = bf16[3,1280,160]{1,2,0:T(8,128)(2,1)S(1)} copy-done((bf16[3,1280,160]{1,2,0:T(8,128)(2,1)S(1)}, bf16[3,1280,160]{1,2,0:T(8,128)(2,1)}, u32[]{:S(2)}) %copy-start) | copy-done | bytes 1228824
  7.0 0.0 copy-start.1
  7.0 1.1 %copy-done.1 = bf16[1280,320]{0,1:T(8,128)(2,1)S(1)} copy-done((bf16[1280,320]{0,1:T(8,128)(2,1)S(1)}, bf16[1280,320]{0,1:T(8,128)(2,1)}, u32[]{:S(2)}) %copy-start.1) | copy-done | bytes 819224
  8.2 0.0 copy-start.2
  8.2 1.1 %copy-done.2 = bf16[320,1280]{1,0:T(8,128)(2,1)S(1)} copy-done((bf16[320,1280]{1,0:T(8,128)(2,1)S(1)}, bf16[320,1280]{1,0:T(8,128)(2,1)}, u32[]{:S(2)}) %copy-start.2) | copy-done | bytes 819224
  9.3 0.0 copy-start.3
  9.3 1.0 %copy-done.3 = bf16[160,1280]{1,0:T(8,128)(2,1)S(1)} copy-done((bf16[160,1280]{1,0:T(8,128)(2,1)S(1)}, bf16[160,1280]{1,0:T(8,128)(2,1)}, u32[]{:S(2)}) %copy-start.3) | copy-done | bytes 409624
  10.3 0.9 %copy-done.4 = bf16[16,3,1280]{2,0,1:T(8,128)(2,1)S(1)} copy-done((bf16[16,3,1280]{2,0,1:T(8,128)(2,1)S(1)}, bf16[16,3,1280]{2,0,1:T(8,128)(2,1)}, u32[]{:S(2)}) %copy-start.4) | copy-done | bytes 122904
  11.2 0.0 copy-start.5
  11.2 0.7 %copy-done.5 = s32[16,3]{0,1:T(4,128)S(1)} copy-done((s32[16,3]{0,1:T(4,128)S(1)}, s32[16,3]{0,1:T(4,128)}, u32[]{:S(2)}) %copy-start.5) | copy-done | bytes 216
  11.9 0.0 copy-start.6
  11.9 0.7 %copy-done.6 = s32[64]{0:T(128)S(1)} copy-done((s32[64]{0:T(128)S(1)}, s32[64]{0:T(128)}, u32[]{:S(2)}) %copy-start.6) | copy-done | bytes 280
  12.5 41.3 %encode.1 = bf16[3,16,1280]{2,1,0:T(8,128)(2,1)S(1)} custom-call(s32[64]{0:T(128)S(1)} %copy-done.6, s32[3,16]{1,0:T(4,128)S(1)} %bitcast.11, bf16[16,1280]{1,0:T(8,128)(2,1)S(1)} %stack.39.vectors, bf16[3,16,1280]{2,1,0:T(8,128)(2,1)S(1)} %bitcast.10, bf16[3,160,1280]{2,1,0:T(8,128)(2,1)S(1)} %bitcast.7, bf16[160,1280]{1,0:T(8,128)(2,1)S(1)} %copy-done.3, ...), custom_call_target="tpu_custom_call" | custom-call | tf_op jit(solution)/shard_map/encode/pallas_call | solution.py:360
  53.9 0.7 %copy.17 = bf16[16,3,1280]{2,0,1:T(8,128)(2,1)} copy(bf16[16,3,1280]{2,0,1:T(8,128)(2,1)S(1)} %bitcast.9) | data formatting | bytes 245760
  (6 shorter events, 0.0 us)
Async XLA Ops:
  5.7 1.3 %copy-start = (bf16[3,1280,160]{1,2,0:T(8,128)(2,1)S(1)}, bf16[3,1280,160]{1,2,0:T(8,128)(2,1)}, u32[]{:S(2)}) copy-start(bf16[3,1280,160]{1,2,0:T(8,128)(2,1)} %param.20) | copy-start | bytes 3686404
  7.0 1.1 %copy-start.1 = (bf16[1280,320]{0,1:T(8,128)(2,1)S(1)}, bf16[1280,320]{0,1:T(8,128)(2,1)}, u32[]{:S(2)}) copy-start(bf16[1280,320]{0,1:T(8,128)(2,1)} %param.26) | copy-start | bytes 2457604
  8.2 1.1 %copy-start.2 = (bf16[320,1280]{1,0:T(8,128)(2,1)S(1)}, bf16[320,1280]{1,0:T(8,128)(2,1)}, u32[]{:S(2)}) copy-start(bf16[320,1280]{1,0:T(8,128)(2,1)} %fc2_weight.1) | copy-start | bytes 2457604
  9.3 1.0 %copy-start.3 = (bf16[160,1280]{1,0:T(8,128)(2,1)S(1)}, bf16[160,1280]{1,0:T(8,128)(2,1)}, u32[]{:S(2)}) copy-start(bf16[160,1280]{1,0:T(8,128)(2,1)} %proj_weight.1) | copy-start | bytes 1228804
  10.3 0.9 %copy-start.4 = (bf16[16,3,1280]{2,0,1:T(8,128)(2,1)S(1)}, bf16[16,3,1280]{2,0,1:T(8,128)(2,1)}, u32[]{:S(2)}) copy-start(bf16[16,3,1280]{2,0,1:T(8,128)(2,1)} %param.15) | copy-start | bytes 368644
  11.2 0.7 %copy-start.5 = (s32[16,3]{0,1:T(4,128)S(1)}, s32[16,3]{0,1:T(4,128)}, u32[]{:S(2)}) copy-start(s32[16,3]{0,1:T(4,128)} %param.16) | copy-start | bytes 580
  11.9 0.7 %copy-start.6 = (s32[64]{0:T(128)S(1)}, s32[64]{0:T(128)}, u32[]{:S(2)}) copy-start(s32[64]{0:T(128)} %counts.1) | copy-start | bytes 772

commit v2 on v1

--- a/solution.py
+++ b/solution.py
@@ -46,13 +46,26 @@
 def encode(
     counts,
     window,
-    vectors,
     tiles,
+    ln_gain,
+    ln_bias,
     qkv_weight,
+    qkv_bias,
     proj_weight,
+    proj_bias,
+    mlp_gain,
+    mlp_bias,
     fc1_weight,
+    fc1_bias,
     fc2_weight,
+    fc2_bias,
     out,
+    count_all,
+    window_rows,
+    shifts,
+    bias_qkv,
+    fc1_own,
+    fc1_other,
     vec,
     wqkv,
     wproj,
@@ -69,6 +82,10 @@
     ffn_in,
     done_out,
     done_in,
+    wide_bias,
+    wide_fc1,
+    early_sem,
+    plain_sem,
     load_sem,
     weight_send,
     weight_recv,
@@ -90,52 +107,24 @@
     for peer in beside + around:
         pl.semaphore_signal(barrier, inc=1, device_id=peer, device_id_type=MESH)
 
-    loads = [(tiles, tile_rows), (vectors, vec.at[c])]
-    pushes = [(vectors, vec.at[c])]
-    for which in range(3):
-        for head in range(2):
-            pair = (
-                qkv_weight.at[which, pl.ds(head * HEAD_DIM, HEAD_DIM)],
-                wqkv.at[c, which, head, pl.ds(0, HEAD_DIM)],
-            )
-            loads.append(pair)
-            pushes.append(pair)
-    for head in range(2):
-        pair = (
-            proj_weight.at[pl.ds(head * HEAD_DIM, HEAD_DIM)],
-            wproj.at[c, head, pl.ds(0, HEAD_DIM)],
-        )
-        loads.append(pair)
-        pushes.append(pair)
-    for pair in ((fc1_weight, wfc1.at[c]), (fc2_weight, wfc2.at[c])):
-        loads.append(pair)
-        pushes.append(pair)
-    started = []
-    for i, (src, dst) in enumerate(loads):
-        started.append(pltpu.make_async_copy(src, dst, load_sem.at[i]))
-        started[-1].start()
-
-    gap = jnp.zeros((LANES - HEAD_DIM, D), BF16)
-    for core in range(2):
-        for head in range(2):
-            for which in range(3):
-                wqkv[core, which, head, HEAD_DIM:] = gap
-            wproj[core, head, HEAD_DIM:] = gap
-
-    own_count = counts[d]
-    pair_count = own_count + counts[pd]
-    side = jnp.where(own_count > 0, 0, 1)
-
+    early = []
+    for i, (src, dst) in enumerate(
+        ((tiles, tile_rows), (window, window_rows), (counts, count_all))
+    ):
+        early.append(pltpu.make_async_copy(src, dst, early_sem.at[i]))
+        early[-1].start()
+
+    row, col = iotas((64, 48))
+    inner = row % QUARTER
+    pick = one_hot((inner < 12) & (col == (inner // 4) * 16 + (row // QUARTER) * 4 + inner % 4))
+    early[0].wait()
+    early[1].wait()
     row, col = iotas((16, 16))
     labels = []
     for token in range(3):
-        picked = jnp.where(row == col, window[token : token + 1, :].astype(F32), 0.0)
+        picked = jnp.where(row == col, window_rows[token : token + 1, :].astype(F32), 0.0)
         labels.append(jnp.sum(picked, axis=1, keepdims=True))
     labels = jnp.broadcast_to(jnp.concatenate(labels, axis=0), (48, LANES)).astype(BF16)
-    row, col = iotas((64, 48))
-    inner = row % QUARTER
-    pick = one_hot((inner < 12) & (col == (inner // 4) * 16 + (row // QUARTER) * 4 + inner % 4))
-    started[0].wait()
     features = tile_rows[...].reshape(48, D)
     quarters = matmul(pick, jnp.concatenate([features, labels], axis=1))
     quarter_out[...] = quarters.astype(BF16).reshape(4, QUARTER, WIDE)
@@ -172,10 +161,49 @@
                 peer,
             )
         )
-    pushed = []
-    for i, (src, dst) in enumerate(pushes):
-        pushed.append(remote(src, dst, (weight_send.at[i], weight_recv.at[i]), beside[0]))
+
+    pairs = [(qkv_bias, bias_qkv.at[c]), (fc1_bias, None)]
+    for which in range(3):
+        for head in range(2):
+            pairs.append(
+                (
+                    qkv_weight.at[which, pl.ds(head * HEAD_DIM, HEAD_DIM)],
+                    wqkv.at[c, which, head, pl.ds(0, HEAD_DIM)],
+                )
+            )
+    for head in range(2):
+        pairs.append(
+            (
+                proj_weight.at[pl.ds(head * HEAD_DIM, HEAD_DIM)],
+                wproj.at[c, head, pl.ds(0, HEAD_DIM)],
+            )
+        )
+    pairs += [(fc1_weight, wfc1.at[c]), (fc2_weight, wfc2.at[c])]
+    pushed, loaded = [], []
+    for i, (src, dst) in enumerate(pairs):
+        there, here = (fc1_other, fc1_own) if dst is None else (dst, dst)
+        pushed.append(remote(src, there, (weight_send.at[i], weight_recv.at[i]), beside[0]))
+        loaded.append(pltpu.make_async_copy(src, here, load_sem.at[i]))
+        loaded[-1].start()
     sent += lends + pushed
+    plain = []
+    for i, src in enumerate((ln_gain, ln_bias, proj_bias, mlp_gain, mlp_bias, fc2_bias)):
+        plain.append(pltpu.make_async_copy(src, shifts[i], plain_sem.at[i]))
+        plain[-1].start()
+
+    gap = jnp.zeros((LANES - HEAD_DIM, D), BF16)
+    for core in range(2):
+        for head in range(2):
+            for which in range(3):
+                wqkv[core, which, head, HEAD_DIM:] = gap
+            wproj[core, head, HEAD_DIM:] = gap
+    early[2].wait()
+    own_count = count_all[d]
+    pair_count = own_count + count_all[pd]
+    side = jnp.where(own_count > 0, 0, 1)
+    for i, copy in enumerate(plain):
+        copy.wait()
+        vec[i : i + 1, :] = shifts[i][...].astype(F32).reshape(1, D)
     for copy in lends:
         copy.wait_recv()
 
@@ -187,10 +215,8 @@
     mine = matmul(pick, quarter_in[...].reshape(64, WIDE))
     rows_in = mine[:, :D]
 
-    started[1].wait()
-
     def vector(i):
-        return vec[c, i : i + 1, :].astype(F32)
+        return vec[i : i + 1, :]
 
     def spread(buffer, phase):
         copies = []
@@ -238,9 +264,18 @@
     normed_all[y] = jnp.concatenate([normed, mine[:, D:].astype(BF16)], axis=1)
     copies = spread(normed_all, 0)
 
-    for copy in started[2:]:
+    for copy in loaded:
         copy.wait()
-    for copy in pushed[:7]:
+    for copy in pushed[:2]:
+        copy.wait_recv()
+    zero = jnp.zeros((1, LANES - HEAD_DIM), F32)
+    pieces = []
+    for core in range(2):
+        for which in range(3):
+            bias = bias_qkv[core, which : which + 1, :].astype(F32)
+            pieces += [bias[:, :HEAD_DIM], zero, bias[:, HEAD_DIM:], zero]
+    wide_bias[...] = jnp.concatenate(pieces, axis=1)
+    for copy in pushed[2:8]:
         copy.wait_recv()
     arrive(copies)
 
@@ -250,10 +285,7 @@
     marks = one_hot(lane == key)
     same = matmul_t(marks, marks) > 0.5
     width = 6 * LANES
-    qkv_bias = jnp.concatenate(
-        [vec[core, 6:7, :width].astype(F32) for core in range(2)], axis=1
-    )
-    qkv = matmul_t(everything[:, :D], wqkv[...].reshape(2 * width, D)) + qkv_bias
+    qkv = matmul_t(everything[:, :D], wqkv[...].reshape(2 * width, D)) + wide_bias[...]
     qkv = qkv.astype(BF16)
     scale = 1.0 / (float(HEAD_DIM) ** 0.5)
     attended = []
@@ -268,7 +300,7 @@
             weights = weights / jnp.sum(weights, axis=1, keepdims=True)
             attended.append(matmul(weights.astype(BF16), values).astype(BF16))
     attended = jnp.concatenate(attended, axis=1)
-    for copy in pushed[7:9]:
+    for copy in pushed[8:10]:
         copy.wait_recv()
     mixed_part = matmul(attended, wproj[...].reshape(4 * LANES, D))
     part_out[...] = mixed_part.reshape(CHIPS, ROWS, D).astype(BF16)
@@ -278,12 +310,16 @@
     mixed = (total(part_in) + vector(2) + rows_in).astype(BF16).astype(F32)
     normed2_all[y] = normalize(mixed, vector(3), vector(4))
     copies = spread(normed2_all, 2)
-    for copy in pushed[9:]:
+    for copy in pushed[10:]:
         copy.wait_recv()
+    own_bias = fc1_own[...].astype(F32).reshape(1, 320)
+    other_bias = fc1_other[...].astype(F32).reshape(1, 320)
+    wide_fc1[...] = jnp.concatenate(
+        [jnp.where(c == 0, own_bias, other_bias), jnp.where(c == 0, other_bias, own_bias)], axis=1
+    )
     arrive(copies)
 
-    fc1_bias = jnp.concatenate([vec[core, 7:8, :320].astype(F32) for core in range(2)], axis=1)
-    lifted = matmul_t(gathered(normed2_all), wfc1[...].reshape(640, D)) + fc1_bias
+    lifted = matmul_t(gathered(normed2_all), wfc1[...].reshape(640, D)) + wide_fc1[...]
     hidden = (lifted * jax.nn.sigmoid(1.702 * lifted)).astype(BF16)
     ffn_part = matmul(hidden, wfc2[...].reshape(640, D))
     ffn_out[...] = ffn_part.reshape(CHIPS, ROWS, D).astype(BF16)
@@ -341,29 +377,21 @@
     fc2_weight,
     fc2_bias,
 ):
-    heads_bias = jnp.pad(qkv_bias.reshape(6, HEAD_DIM), ((0, 0), (0, LANES - HEAD_DIM)))
-    vectors = jnp.stack(
-        [
-            ln_gain,
-            ln_bias,
-            proj_bias,
-            mlp_gain,
-            mlp_bias,
-            fc2_bias,
-            jnp.pad(heads_bias.reshape(768), (0, D - 768)),
-            jnp.pad(fc1_bias, (0, D - 320)),
-        ]
-        + [jnp.zeros((D,), BF16)] * 8
-    )
     vmem = pl.BlockSpec(memory_space=pltpu.VMEM)
     hbm = pl.BlockSpec(memory_space=pltpu.HBM)
     encoded = pl.pallas_call(
         encode,
         out_shape=jax.ShapeDtypeStruct((3, 16, D), BF16),
-        in_specs=[pl.BlockSpec(memory_space=pltpu.SMEM), vmem, hbm, hbm, hbm, hbm, hbm, hbm],
+        in_specs=[hbm] * 15,
         out_specs=vmem,
         scratch_shapes=[
-            pltpu.VMEM((2, 16, D), BF16),
+            pltpu.SMEM((64,), jnp.int32),
+            pltpu.VMEM((3, 16), jnp.int32),
+            [pltpu.VMEM((D,), BF16)] * 6,
+            pltpu.VMEM((2, 3, 160), BF16),
+            pltpu.VMEM((320,), BF16),
+            pltpu.VMEM((320,), BF16),
+            pltpu.VMEM((8, D), F32),
             pltpu.VMEM((2, 3, 2, LANES, D), BF16),
             pltpu.VMEM((2, 2, LANES, D), BF16),
             pltpu.VMEM((2, 320, D), BF16),
@@ -379,9 +407,13 @@
             pltpu.VMEM((CHIPS, ROWS, D), BF16),
             pltpu.VMEM((2, QUARTER, D), BF16),
             pltpu.VMEM((2, 2, QUARTER, D), BF16),
+            pltpu.VMEM((1, 12 * LANES), F32),
+            pltpu.VMEM((1, 640), F32),
+            pltpu.SemaphoreType.DMA((3,)),
+            pltpu.SemaphoreType.DMA((6,)),
             pltpu.SemaphoreType.DMA((12,)),
-            pltpu.SemaphoreType.DMA((11,)),
-            pltpu.SemaphoreType.DMA((11,)),
+            pltpu.SemaphoreType.DMA((12,)),
+            pltpu.SemaphoreType.DMA((12,)),
             pltpu.SemaphoreType.DMA((3,)),
             pltpu.SemaphoreType.DMA((3,)),
             pltpu.SemaphoreType.DMA((4, 3)),
@@ -390,18 +422,25 @@
             pltpu.SemaphoreType.DMA((3,)),
         ],
         compiler_params=pltpu.CompilerParams(
-            collective_id=0, has_side_effects=True, vmem_limit_bytes=48 * 2**20
+            collective_id=0, has_side_effects=True, vmem_limit_bytes=64 * 2**20
         ),
         name="encode",
     )(
         counts,
         jnp.transpose(window_ids),
-        vectors,
         jnp.transpose(tiles, (1, 0, 2)),
+        ln_gain,
+        ln_bias,
         jnp.swapaxes(qkv_weight, 1, 2),
+        qkv_bias,
         proj_weight,
+        proj_bias,
+        mlp_gain,
+        mlp_bias,
         jnp.transpose(fc1_weight),
+        fc1_bias,
         fc2_weight,
+        fc2_bias,
     )
     return jnp.transpose(encoded, (1, 0, 2))
 

time: 55.1 us -> 42.9 us (0.78)
  local copies, waits for them, and re-layouts: 13.2 us -> 1.56 us
    unnamed x15 -> x1, local copies, waits for them, and re-layouts: 7.46 us -> 1.56 us
    another operation x10 -> x0, local copies, waits for them, and re-layouts: 4.24 us -> none  [on_device(): jnp.stack([ln_gain, ln_bias, proj_bias, mlp_gain, mlp_bias, fc2_bias, jnp...]
    reshape x2 -> x0, local copies, waits for them, and re-layouts: 0.77 us -> none  [the longest x1 0.76 us: on_device(): qkv_bias.reshape(6, HEAD_DIM)]
    pad x2 -> x0, local copies, waits for them, and re-layouts: 0.69 us -> none  [the longest x1 0.69 us: on_device(): jnp.pad(fc1_bias, (0, D - 320))]
where the time goes in v2:
time: 42.9 us; the launch traced here: 42.8 us
  Pallas kernels  41.2 us (96%)
  local copies, waits for them, and re-layouts  1.56 us (4%)
    pallas_call x1, Pallas kernels, on_device(): pl.pallas_call(encode, out_shape=jax.ShapeDtypeStruct((3, 16, D), BF16),...  41.2 us
    unnamed x1, local copies, waits for them, and re-layouts  1.56 us

profile of v2, /device:TPU:1, one launch (start us, length us, event | category | flops | bytes accessed | tf_op | source)
XLA Modules:
  0.0 42.8 jit_solution(13286007031432196403)
XLA Ops:
  0.0 41.2 %encode.1 = bf16[3,16,1280]{2,1,0:T(8,128)(2,1)} custom-call(s32[64]{0:T(128)} %counts.1, s32[3,16]{1,0:T(4,128)} %bitcast.9, bf16[3,16,1280]{2,1,0:T(8,128)(2,1)} %bitcast.8, bf16[1280]{0:T(1024)(128)(2,1)} %ln_gain.1, bf16[1280]{0:T(1024)(128)(2,1)} %ln_bias.1, bf16[3,160,1280]{2,1,0:T(8,128)(2,1)} %bitcast.5, bf16[3,160]{1,0:T(4,128)(2,1)} %qkv_bias.1, ...), custom_call_target="tpu_custom_call" | custom-call | tf_op jit(solution)/shard_map/encode/pallas_call | solution.py:382
  41.2 1.6 %copy.17 = bf16[16,3,1280]{2,0,1:T(8,128)(2,1)} copy(bf16[16,3,1280]{2,0,1:T(8,128)(2,1)} %bitcast.7) | data formatting | bytes 245760

commit v3 on v2

v3 whole, which is shorter than its diff:
```python
import jax
import jax.numpy as jnp
from jax import lax
from jax.experimental import pallas as pl
from jax.experimental.pallas import tpu as pltpu
from jax.sharding import PartitionSpec as P

D = 1280
HEAD_DIM = 80
LANES = 128
WIDE = D + LANES
QUARTER = 16
ROWS = 24
CHIPS = 4
GROUP = CHIPS * ROWS
CHUNKS = 2
MESH = pl.DeviceIdType.MESH
F32 = jnp.float32
BF16 = jnp.bfloat16


def matmul(left, right):
    return jnp.dot(left, right, preferred_element_type=F32)


def matmul_t(left, right):
    return lax.dot_general(left, right, (((1,), (1,)), ((), ())), preferred_element_type=F32)


def normalize(rows, gain, shift):
    centred = rows - jnp.mean(rows, axis=-1, keepdims=True)
    variance = jnp.mean(centred * centred, axis=-1, keepdims=True)
    return (centred * lax.rsqrt(variance + 1e-06) * gain + shift).astype(BF16)


def iotas(shape):
    return (
        lax.broadcasted_iota(jnp.int32, shape, 0),
        lax.broadcasted_iota(jnp.int32, shape, 1),
    )


def one_hot(flags):
    return jnp.where(flags, 1.0, 0.0).astype(BF16)


def encode(
    counts,
    window,
    tiles,
    ln_gain,
    ln_bias,
    qkv_weight,
    qkv_bias,
    proj_weight,
    proj_bias,
    mlp_gain,
    mlp_bias,
    fc1_weight,
    fc1_bias,
    fc2_weight,
    fc2_bias,
    out,
    count_all,
    window_rows,
    shifts,
    bias_qkv,
    fc1_own,
    fc1_other,
    vec,
    wide_bias,
    wide_fc1,
    wqkv,
    wproj,
    wfc1,
    wfc2,
    tile_rows,
    quarter_out,
    quarter_in,
    kept,
    normed_all,
    part_out,
    part_in,
    normed2_all,
    ffn_out,
    ffn_in,
    done_out,
    done_in,
    early_sem,
    plain_sem,
    load_sem,
    weight_send,
    weight_recv,
    swap_send,
    swap_recv,
    ring_send,
    ring_recv,
    back_send,
    back_recv,
):
    d, t = lax.axis_index("dp"), lax.axis_index("tensor")
    y, c = t // 2, t % 2
    other = 1 - c
    beside = (d, y * 2 + other)
    around = [(d, ((y + k) % CHIPS) * 2 + c) for k in (2, 1, 3)]

    barrier = pltpu.get_barrier_semaphore()
    for peer in around + [beside]:
        pl.semaphore_signal(barrier, inc=1, device_id=peer, device_id_type=MESH)

    early = []
    for i, (src, dst) in enumerate(
        ((tiles, tile_rows), (window, window_rows), (counts, count_all))
    ):
        early.append(pltpu.make_async_copy(src, dst, early_sem.at[i]))
        early[-1].start()

    row, col = iotas((64, 48))
    inner = row % QUARTER
    pick = one_hot((inner < 12) & (col == (inner // 4) * 16 + (row // QUARTER) * 4 + inner % 4))
    early[1].wait()
    row, col = iotas((16, 16))
    labels = []
    for token in range(3):
        picked = jnp.where(row == col, window_rows[token : token + 1, :].astype(F32), 0.0)
        labels.append(jnp.sum(picked, axis=1, keepdims=True))
    labels = jnp.broadcast_to(jnp.concatenate(labels, axis=0), (48, LANES)).astype(BF16)
    early[0].wait()
    features = tile_rows[...].reshape(48, D)
    quarters = matmul(pick, jnp.concatenate([features, labels], axis=1))
    quarter_out[...] = quarters.astype(BF16).reshape(4, QUARTER, WIDE)

    pl.semaphore_wait(barrier, len(around) + 1)

    def remote(src, dst, send, recv, peer):
        copy = pltpu.make_async_remote_copy(
            src_ref=src,
            dst_ref=dst,
            send_sem=send,
            recv_sem=recv,
            device_id=peer,
            device_id_type=MESH,
        )
        copy.start()
        return copy

    sent = []
    swaps = []
    for k in range(CHUNKS):
        swaps.append(
            remote(
                quarter_out.at[2 * other + k],
                quarter_in.at[c, k],
                swap_send.at[k],
                swap_recv.at[k],
                beside,
            )
        )
    pairs = [(qkv_bias, bias_qkv.at[c]), (fc1_bias, None)]
    for which in range(3):
        for head in range(2):
            pairs.append(
                (
                    qkv_weight.at[which, pl.ds(head * HEAD_DIM, HEAD_DIM)],
                    wqkv.at[c, which, head, pl.ds(0, HEAD_DIM)],
                )
            )
    for head in range(2):
        pairs.append(
            (
                proj_weight.at[pl.ds(head * HEAD_DIM, HEAD_DIM)],
                wproj.at[c, head, pl.ds(0, HEAD_DIM)],
            )
        )
    pairs += [(fc1_weight, wfc1.at[c]), (fc2_weight, wfc2.at[c])]
    pushed, loaded = [], []
    for i, (src, dst) in enumerate(pairs):
        there, here = (fc1_other, fc1_own) if dst is None else (dst, dst)
        pushed.append(remote(src, there, weight_send.at[i], weight_recv.at[i], beside))
        loaded.append(pltpu.make_async_copy(src, here, load_sem.at[i]))
        loaded[-1].start()
    sent += swaps + pushed
    plain = []
    for i, src in enumerate((ln_gain, ln_bias, proj_bias, mlp_gain, mlp_bias, fc2_bias)):
        plain.append(pltpu.make_async_copy(src, shifts[i], plain_sem.at[i]))
        plain[-1].start()

    def vector(i):
        return vec[i : i + 1, :]

    def lay_out(i):
        plain[i].wait()
        vec[i : i + 1, :] = shifts[i][...].astype(F32).reshape(1, D)

    for k in range(CHUNKS):
        quarter_in[c, k] = quarter_out[2 * c + k]
    lay_out(0)
    lay_out(1)

    def spread(buffer, phase, k):
        copies = []
        for i, peer in enumerate(around):
            copies.append(
                remote(
                    buffer.at[k, y],
                    buffer.at[k, y],
                    ring_send.at[phase, k, i],
                    ring_recv.at[phase, k, i],
                    peer,
                )
            )
        return copies

    def scatter(source, target, phase, k):
        copies = []
        for i, peer in enumerate(around):
            copies.append(
                remote(
                    source.at[k, peer[1] // 2],
                    target.at[k, y],
                    ring_send.at[phase, k, i],
                    ring_recv.at[phase, k, i],
                    peer,
                )
            )
        target[k, y] = source[k, y]
        return copies

    def arrive(copies):
        for copy in copies:
            copy.wait_recv()
        sent.extend(copies)

    def gathered(buffer, k):
        return jnp.concatenate(
            [buffer[k, i].astype(F32) for i in range(CHIPS)], axis=0
        ).astype(BF16)

    def total(buffer, k):
        out_sum = buffer[k, 0].astype(F32)
        for i in range(1, CHIPS):
            out_sum = out_sum + buffer[k, i].astype(F32)
        return out_sum

    row, col = iotas((ROWS, 2 * QUARTER))
    inner = col % QUARTER
    pick = one_hot((inner < 12) & (row == (col // QUARTER) * 12 + inner))
    moving = []
    for k in range(CHUNKS):
        swaps[k].wait_recv()
        both = jnp.concatenate([quarter_in[0, k], quarter_in[1, k]], axis=0)
        mine = matmul(pick, both)
        kept[k] = mine[:, :D]
        normed = normalize(mine[:, :D], vector(0), vector(1))
        normed_all[k, y] = jnp.concatenate([normed, mine[:, D:].astype(BF16)], axis=1)
        moving.append(spread(normed_all, 0, k))

    for i in range(2, 6):
        lay_out(i)
    gap = jnp.zeros((LANES - HEAD_DIM, D), BF16)
    for core in range(2):
        for head in range(2):
            for which in range(3):
                wqkv[core, which, head, HEAD_DIM:] = gap
            wproj[core, head, HEAD_DIM:] = gap
    for copy in loaded:
        copy.wait()
    for copy in pushed[:2]:
        copy.wait_recv()
    zero = jnp.zeros((1, LANES - HEAD_DIM), F32)
    pieces = []
    for core in range(2):
        for which in range(3):
            bias = bias_qkv[core, which : which + 1, :].astype(F32)
            pieces += [bias[:, :HEAD_DIM], zero, bias[:, HEAD_DIM:], zero]
    wide_bias[...] = jnp.concatenate(pieces, axis=1)
    own_bias = fc1_own[...].astype(F32).reshape(1, 320)
    other_bias = fc1_other[...].astype(F32).reshape(1, 320)
    wide_fc1[...] = jnp.concatenate(
        [jnp.where(c == 0, own_bias, other_bias), jnp.where(c == 0, other_bias, own_bias)], axis=1
    )
    for copy in pushed[2:10]:
        copy.wait_recv()
    early[2].wait()
    own_count = count_all[d]

    width = 6 * LANES
    scale = 1.0 / (float(HEAD_DIM) ** 0.5)
    summing = []
    for k in range(CHUNKS):
        arrive(moving[k])
        everything = gathered(normed_all, k)
        row, lane = iotas((GROUP, LANES))
        key = everything[:, D:].astype(F32).astype(jnp.int32) + 4 * (row % 4)
        marks = one_hot(lane == key)
        same = matmul_t(marks, marks) > 0.5
        qkv = matmul_t(everything[:, :D], wqkv[...].reshape(2 * width, D)) + wide_bias[...]
        qkv = qkv.astype(BF16)
        attended = []
        for core in range(2):
            for head in range(2):
                base = core * width + head * LANES
                query = qkv[:, base : base + LANES]
                keys = qkv[:, base + 2 * LANES : base + 3 * LANES]
                values = qkv[:, base + 4 * LANES : base + 5 * LANES]
                scores = matmul_t(query, keys) * scale
                weights = jnp.where(same, jnp.exp(scores), 0.0)
                weights = weights / jnp.sum(weights, axis=1, keepdims=True)
                attended.append(matmul(weights.astype(BF16), values).astype(BF16))
        attended = jnp.concatenate(attended, axis=1)
        mixed_part = matmul(attended, wproj[...].reshape(4 * LANES, D))
        part_out[k] = mixed_part.reshape(CHIPS, ROWS, D).astype(BF16)
        summing.append(scatter(part_out, part_in, 1, k))

    moving = []
    for k in range(CHUNKS):
        arrive(summing[k])
        mixed = (total(part_in, k) + vector(2) + kept[k]).astype(BF16).astype(F32)
        kept[k] = mixed
        normed2_all[k, y] = normalize(mixed, vector(3), vector(4))
        moving.append(spread(normed2_all, 2, k))

    for copy in pushed[10:]:
        copy.wait_recv()
    summing = []
    for k in range(CHUNKS):
        arrive(moving[k])
        lifted = matmul_t(gathered(normed2_all, k), wfc1[...].reshape(640, D)) + wide_fc1[...]
        hidden = (lifted * jax.nn.sigmoid(1.702 * lifted)).astype(BF16)
        ffn_part = matmul(hidden, wfc2[...].reshape(640, D))
        ffn_out[k] = ffn_part.reshape(CHIPS, ROWS, D).astype(BF16)
        summing.append(scatter(ffn_out, ffn_in, 3, k))

    row, col = iotas((2 * QUARTER, ROWS))
    inner = row % QUARTER
    pick = one_hot((inner < 12) & (col == (row // QUARTER) * 12 + inner))
    row, col = iotas((ROWS, D))
    backs = []
    for k in range(CHUNKS):
        arrive(summing[k])
        slot = 8 * c + 4 * k + row % 4
        encoded = total(ffn_in, k) + vector(5) + kept[k]
        encoded = jnp.where(slot < own_count, encoded, 0.0).astype(BF16)
        done_out[k] = matmul(pick, encoded).astype(BF16).reshape(2, QUARTER, D)
        backs.append(
            remote(
                done_out.at[k, other],
                done_in.at[c, k],
                back_send.at[k],
                back_recv.at[k],
                beside,
            )
        )
        done_in[c, k] = done_out[k, c]
    arrive(backs)

    row, col = iotas((48, 64))
    inner = col % QUARTER
    pick = one_hot(
        (inner < 12) & (row == (inner // 4) * 16 + (col // QUARTER) * 4 + inner % 4)
    )
    out[...] = matmul(pick, done_in[...].reshape(64, D)).astype(BF16).reshape(3, 16, D)
    for copy in sent:
        copy.wait_send()


def on_device(
    tiles,
    window_ids,
    counts,
    ln_gain,
    ln_bias,
    qkv_weight,
    qkv_bias,
    proj_weight,
    proj_bias,
    mlp_gain,
    mlp_bias,
    fc1_weight,
    fc1_bias,
    fc2_weight,
    fc2_bias,
):
    operands = (
        counts,
        jnp.transpose(window_ids),
        jnp.transpose(tiles, (1, 0, 2)),
        ln_gain,
        ln_bias,
        jnp.swapaxes(qkv_weight, 1, 2),
        qkv_bias,
        proj_weight,
        proj_bias,
        mlp_gain,
        mlp_bias,
        jnp.transpose(fc1_weight),
        fc1_bias,
        fc2_weight,
        fc2_bias,
    )
    encoded = pl.pallas_call(
        encode,
        out_shape=pltpu.VMEM((3, 16, D), BF16),
        in_specs=[pl.BlockSpec(memory_space=pltpu.HBM)] * len(operands),
        out_specs=pl.BlockSpec(memory_space=pltpu.VMEM),
        scratch_shapes=[
            pltpu.SMEM((64,), jnp.int32),
            pltpu.VMEM((3, 16), jnp.int32),
            [pltpu.VMEM((D,), BF16)] * 6,
            pltpu.VMEM((2, 3, 160), BF16),
            pltpu.VMEM((320,), BF16),
            pltpu.VMEM((320,), BF16),
            pltpu.VMEM((8, D), F32),
            pltpu.VMEM((1, 12 * LANES), F32),
            pltpu.VMEM((1, 640), F32),
            pltpu.VMEM((2, 3, 2, LANES, D), BF16),
            pltpu.VMEM((2, 2, LANES, D), BF16),
            pltpu.VMEM((2, 320, D), BF16),
            pltpu.VMEM((2, 320, D), BF16),
            pltpu.VMEM((3, 16, D), BF16),
            pltpu.VMEM((4, QUARTER, WIDE), BF16),
            pltpu.VMEM((2, CHUNKS, QUARTER, WIDE), BF16),
            pltpu.VMEM((CHUNKS, ROWS, D), F32),
            pltpu.VMEM((CHUNKS, CHIPS, ROWS, WIDE), BF16),
            pltpu.VMEM((CHUNKS, CHIPS, ROWS, D), BF16),
            pltpu.VMEM((CHUNKS, CHIPS, ROWS, D), BF16),
            pltpu.VMEM((CHUNKS, CHIPS, ROWS, D), BF16),
            pltpu.VMEM((CHUNKS, CHIPS, ROWS, D), BF16),
            pltpu.VMEM((CHUNKS, CHIPS, ROWS, D), BF16),
            pltpu.VMEM((CHUNKS, 2, QUARTER, D), BF16),
            pltpu.VMEM((2, CHUNKS, QUARTER, D), BF16),
            pltpu.SemaphoreType.DMA((3,)),
            pltpu.SemaphoreType.DMA((6,)),
            pltpu.SemaphoreType.DMA((12,)),
            pltpu.SemaphoreType.DMA((12,)),
            pltpu.SemaphoreType.DMA((12,)),
            pltpu.SemaphoreType.DMA((CHUNKS,)),
            pltpu.SemaphoreType.DMA((CHUNKS,)),
            pltpu.SemaphoreType.DMA((4, CHUNKS, 3)),
            pltpu.SemaphoreType.DMA((4, CHUNKS, 3)),
            pltpu.SemaphoreType.DMA((CHUNKS,)),
            pltpu.SemaphoreType.DMA((CHUNKS,)),
        ],
        compiler_params=pltpu.CompilerParams(
            collective_id=0, has_side_effects=True, vmem_limit_bytes=48 * 2**20
        ),
        name="encode",
    )(*(pltpu.with_memory_space_constraint(operand, pltpu.HBM) for operand in operands))
    return jnp.transpose(encoded, (1, 0, 2))


def solution(mesh):
    placed = (
        P("dp", "tensor", None),
        P("dp", "tensor"),
        P(),
        P(),
        P(),
        P(None, None, "tensor"),
        P(None, "tensor"),
        P("tensor", None),
        P(),
        P(),
        P(),
        P(None, "tensor"),
        P("tensor"),
        P("tensor", None),
        P(),
    )
    return jax.shard_map(
        on_device, mesh=mesh, in_specs=placed, out_specs=P("dp", "tensor", None), check_vma=False
    )
```

time: 42.9 us -> 41.6 us (0.970)
  local copies, waits for them, and re-layouts: 1.56 us -> 0.65 us
    unnamed x1, local copies, waits for them, and re-layouts: 1.56 us -> 0.65 us
where the time goes in v3:
time: 41.6 us; the launch traced here: 41.4 us
  Pallas kernels  40.8 us (98%)
  local copies, waits for them, and re-layouts  0.65 us (2%)
    pallas_call x1, Pallas kernels, on_device(): pl.pallas_call(encode, out_shape=pltpu.VMEM((3, 16, D), BF16), in_specs=[...  40.8 us

profile of v3, /device:TPU:1, one launch (start us, length us, event | category | flops | bytes accessed | tf_op | source)
XLA Modules:
  0.0 41.4 jit_solution(15922527785951656878)
XLA Ops:
  0.0 40.8 %encode.1 = bf16[3,16,1280]{2,1,0:T(8,128)(2,1)S(1)} custom-call(s32[64]{0:T(128)} %counts.1, s32[3,16]{1,0:T(4,128)} %bitcast.9, bf16[3,16,1280]{2,1,0:T(8,128)(2,1)} %bitcast.8, bf16[1280]{0:T(1024)(128)(2,1)} %ln_gain.1, bf16[1280]{0:T(1024)(128)(2,1)} %ln_bias.1, bf16[3,160,1280]{2,1,0:T(8,128)(2,1)} %bitcast.6, bf16[3,160]{1,0:T(4,128)(2,1)} %qkv_bias.1, ...), custom_call_target="tpu_custom_call" | custom-call | tf_op jit(solution)/shard_map/encode/pallas_call | solution.py:401
  40.8 0.7 %copy.17 = bf16[16,3,1280]{2,0,1:T(8,128)(2,1)} copy(bf16[16,3,1280]{2,0,1:T(8,128)(2,1)S(1)} %bitcast.5) | data formatting | bytes 245760

commit v4 on v3

v4 whole, which is shorter than its diff:
```python
import jax
import jax.numpy as jnp
from jax import lax
from jax.experimental import pallas as pl
from jax.experimental.pallas import tpu as pltpu
from jax.sharding import PartitionSpec as P

D = 1280
HEAD_DIM = 80
LANES = 128
WIDE = D + LANES
QUARTER = 16
ROWS = 24
CHIPS = 4
GROUP = CHIPS * ROWS
CHUNKS = 2
HALF = 32
HEAD_LANES = 384
MESH = pl.DeviceIdType.MESH
F32 = jnp.float32
BF16 = jnp.bfloat16


def matmul(left, right):
    return jnp.dot(left, right, preferred_element_type=F32)


def matmul_t(left, right):
    return lax.dot_general(left, right, (((1,), (1,)), ((), ())), preferred_element_type=F32)


def normalize(rows, gain, shift):
    centred = rows - jnp.mean(rows, axis=-1, keepdims=True)
    variance = jnp.mean(centred * centred, axis=-1, keepdims=True)
    return (centred * lax.rsqrt(variance + 1e-06) * gain + shift).astype(BF16)


def iotas(shape):
    return (
        lax.broadcasted_iota(jnp.int32, shape, 0),
        lax.broadcasted_iota(jnp.int32, shape, 1),
    )


def one_hot(flags):
    return jnp.where(flags, 1.0, 0.0).astype(BF16)


def encode(
    counts,
    window,
    tiles,
    ln_gain,
    ln_bias,
    qkv_weight,
    qkv_bias,
    proj_weight,
    proj_bias,
    mlp_gain,
    mlp_bias,
    fc1_weight,
    fc1_bias,
    fc2_weight,
    fc2_bias,
    out,
    count_all,
    window_rows,
    shifts,
    bias_qkv,
    fc1_own,
    fc1_other,
    vec,
    wide_bias,
    wide_fc1,
    wqkv,
    wproj,
    wfc1,
    wfc2,
    tile_rows,
    quarter_out,
    quarter_in,
    kept,
    lent_out,
    lent_in,
    normed_all,
    normed_lent,
    lent_block,
    part_out,
    part_in,
    normed2_all,
    ffn_out,
    ffn_in,
    done_out,
    done_in,
    early_sem,
    plain_sem,
    load_sem,
    weight_send,
    weight_recv,
    swap_send,
    swap_recv,
    lend_send,
    lend_recv,
    ring_send,
    ring_recv,
    back_send,
    back_recv,
):
    d, t = lax.axis_index("dp"), lax.axis_index("tensor")
    y, c = t // 2, t % 2
    other = 1 - c
    beside = (d, y * 2 + other)
    partner = (d + HALF) % (2 * HALF)
    around = [(d, ((y + k) % CHIPS) * 2 + c) for k in (2, 1, 3)]
    across = [(partner, ((y + k) % CHIPS) * 2 + c) for k in (2, 1, 3, 0)]

    barrier = pltpu.get_barrier_semaphore()
    for peer in around + across + [beside]:
        pl.semaphore_signal(barrier, inc=1, device_id=peer, device_id_type=MESH)

    early = []
    for i, (src, dst) in enumerate(
        ((tiles, tile_rows), (window, window_rows), (counts, count_all))
    ):
        early.append(pltpu.make_async_copy(src, dst, early_sem.at[i]))
        early[-1].start()

    row, col = iotas((64, 48))
    inner = row % QUARTER
    pick = one_hot((inner < 12) & (col == (inner // 4) * 16 + (row // QUARTER) * 4 + inner % 4))
    early[1].wait()
    row, col = iotas((16, 16))
    labels = []
    for token in range(3):
        picked = jnp.where(row == col, window_rows[token : token + 1, :].astype(F32), 0.0)
        labels.append(jnp.sum(picked, axis=1, keepdims=True))
    labels = jnp.broadcast_to(jnp.concatenate(labels, axis=0), (48, LANES)).astype(BF16)
    early[0].wait()
    features = tile_rows[...].reshape(48, D)
    quarters = matmul(pick, jnp.concatenate([features, labels], axis=1))
    quarter_out[...] = quarters.astype(BF16).reshape(4, QUARTER, WIDE)

    pl.semaphore_wait(barrier, len(around) + len(across) + 1)

    def remote(src, dst, send, recv, peer):
        copy = pltpu.make_async_remote_copy(
            src_ref=src,
            dst_ref=dst,
            send_sem=send,
            recv_sem=recv,
            device_id=peer,
            device_id_type=MESH,
        )
        copy.start()
        return copy

    sent = []
    swaps = []
    for k in range(CHUNKS):
        swaps.append(
            remote(
                quarter_out.at[other + 2 * k],
                quarter_in.at[c, k],
                swap_send.at[k],
                swap_recv.at[k],
                beside,
            )
        )
    sent += swaps
    plain = []
    for i, src in enumerate((ln_gain, ln_bias, proj_bias, mlp_gain, mlp_bias, fc2_bias)):
        plain.append(pltpu.make_async_copy(src, shifts[i], plain_sem.at[i]))
        plain[-1].start()

    def vector(i):
        return vec[i : i + 1, :]

    def lay_out(i):
        plain[i].wait()
        vec[i : i + 1, :] = shifts[i][...].astype(F32).reshape(1, D)

    for k in range(CHUNKS):
        quarter_in[c, k] = quarter_out[c + 2 * k]
    lay_out(0)
    lay_out(1)

    def spread(buffer, phase, lent=None, landing=None):
        copies = []
        for i in range(CHIPS):
            if lent is not None:
                copies.append(
                    remote(
                        lent,
                        landing.at[y],
                        lend_send.at[phase, i],
                        lend_recv.at[phase, i],
                        across[i],
                    )
                )
            if i < len(around):
                copies.append(
                    remote(
                        buffer.at[y],
                        buffer.at[y],
                        ring_send.at[phase, i],
                        ring_recv.at[phase, i],
                        around[i],
                    )
                )
        return copies

    def scatter(source, target, phase, landing=None):
        copies = []
        for i in range(CHIPS):
            if landing is not None:
                copies.append(
                    remote(
                        source.at[across[i][1] // 2],
                        landing.at[y],
                        lend_send.at[phase, i],
                        lend_recv.at[phase, i],
                        across[i],
                    )
                )
            if i < len(around):
                copies.append(
                    remote(
                        source.at[around[i][1] // 2],
                        target.at[y],
                        ring_send.at[phase, i],
                        ring_recv.at[phase, i],
                        around[i],
                    )
                )
        target[y] = source[y]
        return copies

    def arrive(copies):
        for copy in copies:
            copy.wait_recv()
        sent.extend(copies)

    def gathered(buffer):
        return jnp.concatenate([buffer[i].astype(F32) for i in range(CHIPS)], axis=0)

    def total(buffer):
        out_sum = buffer[0].astype(F32)
        for i in range(1, CHIPS):
            out_sum = out_sum + buffer[i].astype(F32)
        return out_sum

    row, col = iotas((ROWS, 2 * QUARTER))
    inner = col % QUARTER
    pick = one_hot((inner < 12) & (row == (col // QUARTER) * 12 + inner))
    for k in range(CHUNKS):
        swaps[k].wait_recv()
        both = jnp.concatenate([quarter_in[0, k], quarter_in[1, k]], axis=0)
        mine = matmul(pick, both)
        normed = normalize(mine[:, :D], vector(0), vector(1))
        block = jnp.concatenate([normed, mine[:, D:].astype(BF16)], axis=1)
        if k == 0:
            kept[...] = mine[:, :D]
            normed_all[y] = block
        else:
            lent_out[...] = mine[:, :D].astype(BF16)
            lent_block[...] = block
    moving = spread(normed_all, 0, lent_block, normed_lent)
    residual = remote(lent_out, lent_in, swap_send.at[CHUNKS], swap_recv.at[CHUNKS], across[3])

    mine_at = pl.multiple_of(c * 160, 16)
    pairs = [(qkv_bias, bias_qkv.at[c]), (fc1_bias, None)]
    for which, start in enumerate((0, HEAD_LANES, HEAD_LANES + 320)):
        pairs.append((qkv_weight.at[which], wqkv.at[pl.ds(start + mine_at, 160)]))
    pairs.append((proj_weight, wproj.at[pl.ds(64 + mine_at, 160)]))
    pairs += [(fc1_weight, wfc1.at[c]), (fc2_weight, wfc2.at[c])]
    pushed, loaded = [], []
    for i, (src, dst) in enumerate(pairs):
        there, here = (fc1_other, fc1_own) if dst is None else (dst, dst)
        pushed.append(remote(src, there, weight_send.at[i], weight_recv.at[i], beside))
        loaded.append(pltpu.make_async_copy(src, here, load_sem.at[i]))
        loaded[-1].start()
    sent += pushed
    for i in range(2, 6):
        lay_out(i)
    gap = jnp.zeros((64, D), BF16)
    wqkv[320:HEAD_LANES, :] = gap
    wproj[0:64, :] = gap
    for copy in loaded:
        copy.wait()
    for copy in pushed[:2]:
        copy.wait_recv()
    pieces = []
    for which in range(3):
        for core in range(2):
            pieces.append(bias_qkv[core, which : which + 1, :].astype(F32))
        if which == 0:
            pieces.append(jnp.zeros((1, 64), F32))
    wide_bias[...] = jnp.concatenate(pieces, axis=1)
    own_bias = fc1_own[...].astype(F32).reshape(1, 320)
    other_bias = fc1_other[...].astype(F32).reshape(1, 320)
    wide_fc1[...] = jnp.concatenate(
        [jnp.where(c == 0, own_bias, other_bias), jnp.where(c == 0, other_bias, own_bias)], axis=1
    )
    for copy in pushed[2:6]:
        copy.wait_recv()
    early[2].wait()
    own_count = count_all[d]
    owner = own_count > 0

    scale = 1.0 / (float(HEAD_DIM) ** 0.5)
    arrive(moving)
    everything = jnp.where(owner, gathered(normed_all), gathered(normed_lent))
    row, lane = iotas((GROUP, LANES))
    marks = one_hot(lane == everything[:, D:].astype(jnp.int32) + 4 * (row % 4))
    same = matmul_t(marks, marks) > 0.5
    qkv = matmul_t(everything[:, :D].astype(BF16), wqkv[...]) + wide_bias[...]
    qkv = qkv.astype(BF16)
    row, lane = iotas((GROUP, HEAD_LANES))
    query, keys, values = (
        qkv[:, start : start + HEAD_LANES] for start in (0, HEAD_LANES, 2 * HEAD_LANES - LANES)
    )
    heads = [(lane >= HEAD_DIM * j) & (lane < HEAD_DIM * (j + 1)) for j in range(4)]
    query = jnp.concatenate([jnp.where(mask, query, 0.0).astype(BF16) for mask in heads], axis=0)
    scores = matmul_t(query, keys) * scale
    same = jnp.concatenate([same] * 4, axis=0)
    weights = jnp.where(same, jnp.exp(scores), 0.0)
    weights = weights / jnp.sum(weights, axis=1, keepdims=True)
    mixture = matmul(weights.astype(BF16), values)
    attended = jnp.zeros((GROUP, HEAD_LANES), F32)
    for j in range(4):
        mask = (lane >= 64 + HEAD_DIM * j) & (lane < 64 + HEAD_DIM * (j + 1))
        attended = jnp.where(mask, mixture[GROUP * j : GROUP * (j + 1)], attended)
    mixed_part = matmul(attended.astype(BF16), wproj[...])
    part_out[...] = mixed_part.reshape(CHIPS, ROWS, D).astype(BF16)
    summing = scatter(part_out, part_in, 1)
    residual.wait_recv()
    sent.append(residual)
    carried = jnp.where(owner, kept[...], lent_in[...].astype(F32)) + vector(2)
    arrive(summing)

    mixed = (total(part_in) + carried).astype(BF16).astype(F32)
    kept[...] = mixed + vector(5)
    normed2_all[y] = normalize(mixed, vector(3), vector(4))
    moving = spread(normed2_all, 2)
    for copy in pushed[6:]:
        copy.wait_recv()
    arrive(moving)

    lifted = matmul_t(gathered(normed2_all).astype(BF16), wfc1[...].reshape(640, D)) + wide_fc1[...]
    hidden = (lifted * jax.nn.sigmoid(1.702 * lifted)).astype(BF16)
    ffn_part = matmul(hidden, wfc2[...].reshape(640, D))
    for i in range(CHIPS):
        block = ffn_part[ROWS * i : ROWS * (i + 1)] + jnp.where(y == i, kept[...], 0.0)
        ffn_out[i] = block.astype(BF16)
    summing = scatter(ffn_out, ffn_in.at[0], 3, ffn_in.at[1])

    row, col = iotas((2 * QUARTER, ROWS))
    inner = row % QUARTER
    pick = one_hot((inner < 12) & (col == (row // QUARTER) * 12 + inner))
    row, col = iotas((ROWS, D))
    arrive(summing)
    backs = []
    for k in range(CHUNKS):
        slot = 4 * c + 8 * k + row % 4
        encoded = jnp.where(slot < own_count, total(ffn_in.at[k]), 0.0).astype(BF16)
        done_out[k] = matmul(pick, encoded).astype(BF16).reshape(2, QUARTER, D)
        backs.append(
            remote(
                done_out.at[k, other],
                done_in.at[c, k],
                back_send.at[k],
                back_recv.at[k],
                beside,
            )
        )
        done_in[c, k] = done_out[k, c]
    arrive(backs)

    row, col = iotas((48, 64))
    inner = col % QUARTER
    pick = one_hot(
        (inner < 12)
        & (
            row
            == (inner // 4) * 16 + 4 * (col // (2 * QUARTER)) + 8 * (col // QUARTER % 2) + inner % 4
        )
    )
    out[...] = matmul(pick, done_in[...].reshape(64, D)).astype(BF16).reshape(3, 16, D)
    for copy in sent:
        copy.wait_send()


def on_device(
    tiles,
    window_ids,
    counts,
    ln_gain,
    ln_bias,
    qkv_weight,
    qkv_bias,
    proj_weight,
    proj_bias,
    mlp_gain,
    mlp_bias,
    fc1_weight,
    fc1_bias,
    fc2_weight,
    fc2_bias,
):
    operands = (
        counts,
        jnp.transpose(window_ids),
        jnp.transpose(tiles, (1, 0, 2)),
        ln_gain,
        ln_bias,
        jnp.swapaxes(qkv_weight, 1, 2),
        qkv_bias,
        proj_weight,
        proj_bias,
        mlp_gain,
        mlp_bias,
        jnp.transpose(fc1_weight),
        fc1_bias,
        fc2_weight,
        fc2_bias,
    )
    encoded = pl.pallas_call(
        encode,
        out_shape=pltpu.VMEM((3, 16, D), BF16),
        in_specs=[pl.BlockSpec(memory_space=pltpu.HBM)] * len(operands),
        out_specs=pl.BlockSpec(memory_space=pltpu.VMEM),
        scratch_shapes=[
            pltpu.SMEM((64,), jnp.int32),
            pltpu.VMEM((3, 16), jnp.int32),
            [pltpu.VMEM((D,), BF16)] * 6,
            pltpu.VMEM((2, 3, 160), BF16),
            pltpu.VMEM((320,), BF16),
            pltpu.VMEM((320,), BF16),
            pltpu.VMEM((8, D), F32),
            pltpu.VMEM((1, 1024), F32),
            pltpu.VMEM((1, 640), F32),
            pltpu.VMEM((1024, D), BF16),
            pltpu.VMEM((HEAD_LANES, D), BF16),
            pltpu.VMEM((2, 320, D), BF16),
            pltpu.VMEM((2, 320, D), BF16),
            pltpu.VMEM((3, 16, D), BF16),
            pltpu.VMEM((4, QUARTER, WIDE), BF16),
            pltpu.VMEM((2, CHUNKS, QUARTER, WIDE), BF16),
            pltpu.VMEM((ROWS, D), F32),
            pltpu.VMEM((ROWS, D), BF16),
            pltpu.VMEM((ROWS, D), BF16),
            pltpu.VMEM((CHIPS, ROWS, WIDE), BF16),
            pltpu.VMEM((CHIPS, ROWS, WIDE), BF16),
            pltpu.VMEM((ROWS, WIDE), BF16),
            pltpu.VMEM((CHIPS, ROWS, D), BF16),
            pltpu.VMEM((CHIPS, ROWS, D), BF16),
            pltpu.VMEM((CHIPS, ROWS, D), BF16),
            pltpu.VMEM((CHIPS, ROWS, D), BF16),
            pltpu.VMEM((CHUNKS, CHIPS, ROWS, D), BF16),
            pltpu.VMEM((CHUNKS, 2, QUARTER, D), BF16),
            pltpu.VMEM((2, CHUNKS, QUARTER, D), BF16),
            pltpu.SemaphoreType.DMA((3,)),
            pltpu.SemaphoreType.DMA((6,)),
            pltpu.SemaphoreType.DMA((8,)),
            pltpu.SemaphoreType.DMA((8,)),
            pltpu.SemaphoreType.DMA((8,)),
            pltpu.SemaphoreType.DMA((CHUNKS + 1,)),
            pltpu.SemaphoreType.DMA((CHUNKS + 1,)),
            pltpu.SemaphoreType.DMA((4, 4)),
            pltpu.SemaphoreType.DMA((4, 4)),
            pltpu.SemaphoreType.DMA((4, 3)),
            pltpu.SemaphoreType.DMA((4, 3)),
            pltpu.SemaphoreType.DMA((CHUNKS,)),
            pltpu.SemaphoreType.DMA((CHUNKS,)),
        ],
        compiler_params=pltpu.CompilerParams(
            collective_id=0, has_side_effects=True, vmem_limit_bytes=48 * 2**20
        ),
        name="encode",
    )(*(pltpu.with_memory_space_constraint(operand, pltpu.HBM) for operand in operands))
    return jnp.transpose(encoded, (1, 0, 2))


def solution(mesh):
    placed = (
        P("dp", "tensor", None),
        P("dp", "tensor"),
        P(),
        P(),
        P(),
        P(None, None, "tensor"),
        P(None, "tensor"),
        P("tensor", None),
        P(),
        P(),
        P(),
        P(None, "tensor"),
        P("tensor"),
        P("tensor", None),
        P(),
    )
    return jax.shard_map(
        on_device, mesh=mesh, in_specs=placed, out_specs=P("dp", "tensor", None), check_vma=False
    )
```

time: 41.6 us -> 42.3 us (1.017)
  Pallas kernels: 40.8 us -> 41.4 us
    pallas_call x1, Pallas kernels: 40.8 us -> 41.4 us  [on_device(): pl.pallas_call(encode, out_shape=pltpu.VMEM((3, 16, D), BF16), in_specs=[...]
where the time goes in v4:
time: 42.3 us; the launch traced here: 42.1 us
  Pallas kernels  41.4 us (98%)
  local copies, waits for them, and re-layouts  0.65 us (2%)
    pallas_call x1, Pallas kernels, on_device(): pl.pallas_call(encode, out_shape=pltpu.VMEM((3, 16, D), BF16), in_specs=[...  41.4 us

profile of v4, /device:TPU:1, one launch (start us, length us, event | category | flops | bytes accessed | tf_op | source)
XLA Modules:
  0.0 42.1 jit_solution(7866982569285525537)
XLA Ops:
  0.0 41.4 %encode.1 = bf16[3,16,1280]{2,1,0:T(8,128)(2,1)S(1)} custom-call(s32[64]{0:T(128)} %counts.1, s32[3,16]{1,0:T(4,128)} %bitcast.9, bf16[3,16,1280]{2,1,0:T(8,128)(2,1)} %bitcast.8, bf16[1280]{0:T(1024)(128)(2,1)} %ln_gain.1, bf16[1280]{0:T(1024)(128)(2,1)} %ln_bias.1, bf16[3,160,1280]{2,1,0:T(8,128)(2,1)} %bitcast.6, bf16[3,160]{1,0:T(4,128)(2,1)} %qkv_bias.1, ...), custom_call_target="tpu_custom_call" | custom-call | tf_op jit(solution)/shard_map/encode/pallas_call | solution.py:427
  41.4 0.7 %copy.17 = bf16[16,3,1280]{2,0,1:T(8,128)(2,1)} copy(bf16[16,3,1280]{2,0,1:T(8,128)(2,1)S(1)} %bitcast.5) | data formatting | bytes 245760

commit v5 on v3

v5 whole, which is shorter than its diff:
```python
import jax
import jax.numpy as jnp
from jax import lax
from jax.experimental import pallas as pl
from jax.experimental.pallas import tpu as pltpu
from jax.sharding import PartitionSpec as P

D = 1280
HEAD_DIM = 80
CHIPS = 4
SLOTS = 16
HALF = SLOTS // 2
TOKENS = 3
ROWS = TOKENS * HALF
GROUP = CHIPS * ROWS
HEADS = 4
HEAD_LANES = 384
MESH = pl.DeviceIdType.MESH
F32 = jnp.float32
BF16 = jnp.bfloat16


def matmul(left, right):
    return jnp.dot(left, right, preferred_element_type=F32)


def matmul_t(left, right):
    return lax.dot_general(left, right, (((1,), (1,)), ((), ())), preferred_element_type=F32)


def normalize(rows, gain, shift):
    centred = rows - jnp.mean(rows, axis=-1, keepdims=True)
    variance = jnp.mean(centred * centred, axis=-1, keepdims=True)
    return centred * lax.rsqrt(variance + 1e-06) * gain + shift


def iotas(shape):
    return (
        lax.broadcasted_iota(jnp.int32, shape, 0),
        lax.broadcasted_iota(jnp.int32, shape, 1),
    )


def one_hot(flags):
    return jnp.where(flags, 1.0, 0.0).astype(BF16)


def encode(
    counts,
    window,
    tiles,
    ln_gain,
    ln_bias,
    qkv_weight,
    qkv_bias,
    proj_weight,
    proj_bias,
    mlp_gain,
    mlp_bias,
    fc1_weight,
    fc1_bias,
    fc2_weight,
    fc2_bias,
    out,
    count_all,
    window_all,
    label_rows,
    shifts,
    bias_qkv,
    fc1_own,
    fc1_other,
    vec,
    wide_bias,
    wide_fc1,
    wqkv,
    wproj,
    wfc1,
    wfc2,
    tile_rows,
    swap_out,
    raw_out,
    raw_in,
    kept,
    normed_all,
    part_out,
    part_in,
    normed2_all,
    ffn_out,
    ffn_in,
    done_out,
    done_in,
    early_sem,
    plain_sem,
    load_sem,
    weight_send,
    weight_recv,
    label_send,
    label_recv,
    swap_send,
    swap_recv,
    ring_send,
    ring_recv,
):
    d, t = lax.axis_index("dp"), lax.axis_index("tensor")
    y, c = t // 2, t % 2
    other = 1 - c
    beside = (d, y * 2 + other)
    around = [(d, ((y + k) % CHIPS) * 2 + c) for k in (2, 1, 3)]

    barrier = pltpu.get_barrier_semaphore()
    for peer in around + [beside]:
        pl.semaphore_signal(barrier, inc=1, device_id=peer, device_id_type=MESH)

    early = []
    for i, (src, dst) in enumerate(
        ((tiles, tile_rows), (window, window_all.at[t]), (counts, count_all))
    ):
        early.append(pltpu.make_async_copy(src, dst, early_sem.at[i]))
        early[-1].start()
    plain = []
    for i, src in enumerate((ln_gain, ln_bias, proj_bias, mlp_gain, mlp_bias, fc2_bias)):
        plain.append(pltpu.make_async_copy(src, shifts[i], plain_sem.at[i]))
        plain[-1].start()

    def vector(i):
        return vec[i : i + 1, :]

    def lay_out(i):
        plain[i].wait()
        vec[i : i + 1, :] = shifts[i][...].astype(F32).reshape(1, D)

    def halves(rows):
        low = [rows[SLOTS * i : SLOTS * i + HALF] for i in range(TOKENS)]
        high = [rows[SLOTS * i + HALF : SLOTS * (i + 1)] for i in range(TOKENS)]
        low, high = jnp.concatenate(low, axis=0), jnp.concatenate(high, axis=0)
        return jnp.where(c == 0, low, high), jnp.where(c == 0, high, low)

    lay_out(0)
    lay_out(1)
    early[0].wait()
    features = tile_rows[...].astype(F32).reshape(TOKENS * SLOTS, D)
    mine, theirs = halves(normalize(features, vector(0), vector(1)))
    swap_out[...] = theirs.astype(BF16)
    normed_all[1, y] = mine.astype(BF16)

    pl.semaphore_wait(barrier, len(around) + 1)

    def remote(src, dst, send, recv, peer):
        copy = pltpu.make_async_remote_copy(
            src_ref=src,
            dst_ref=dst,
            send_sem=send,
            recv_sem=recv,
            device_id=peer,
            device_id_type=MESH,
        )
        copy.start()
        return copy

    def spread(buffer, phase, k):
        return [
            remote(
                buffer.at[k, y],
                buffer.at[k, y],
                ring_send.at[phase, k, i],
                ring_recv.at[phase, k, i],
                peer,
            )
            for i, peer in enumerate(around)
        ]

    def scatter(source, target, phase, k):
        copies = [
            remote(
                source.at[k, peer[1] // 2],
                target.at[k, y],
                ring_send.at[phase, k, i],
                ring_recv.at[phase, k, i],
                peer,
            )
            for i, peer in enumerate(around)
        ]
        target[k, y] = source[k, y]
        return copies

    sent = []

    def drain():
        while sent:
            sent.pop().wait_send()

    def arrive(copies):
        for copy in copies:
            copy.wait_recv()
        sent.extend(copies)

    def gathered(buffer, k):
        return jnp.concatenate([buffer[k, i].astype(F32) for i in range(CHIPS)], axis=0)

    def total(buffer, k):
        out_sum = buffer[k, 0].astype(F32)
        for i in range(1, CHIPS):
            out_sum = out_sum + buffer[k, i].astype(F32)
        return out_sum

    swap = remote(swap_out, normed_all.at[0, y], swap_send.at[0], swap_recv.at[0], beside)
    direct = spread(normed_all, 0, 1)

    def label(i, of, peer):
        return remote(
            window_all.at[of], window_all.at[of], label_send.at[i], label_recv.at[i], peer
        )

    early[1].wait()
    labels = [label(i, t, peer) for i, peer in enumerate([beside] + around)]
    mine, theirs = halves(features)
    kept[1] = mine
    raw_out[...] = theirs.astype(BF16)
    raw = remote(raw_out, raw_in, swap_send.at[1], swap_recv.at[1], beside)
    swap.wait_recv()
    forwarded = spread(normed_all, 0, 0)
    labels[0].wait_recv()
    labels += [label(4 + i, beside[1], peer) for i, peer in enumerate(around)]

    mine_at = pl.multiple_of(c * 160, 16)
    pairs = [(qkv_bias, bias_qkv.at[c]), (fc1_bias, None)]
    for which, start in enumerate((0, HEAD_LANES, HEAD_LANES + 320)):
        pairs.append((qkv_weight.at[which], wqkv.at[pl.ds(start + mine_at, 160)]))
    pairs.append((proj_weight, wproj.at[pl.ds(64 + mine_at, 160)]))
    pairs += [(fc1_weight, wfc1.at[c]), (fc2_weight, wfc2.at[c])]
    pushed, loaded = [], []
    for i, (src, dst) in enumerate(pairs):
        there, here = (fc1_other, fc1_own) if dst is None else (dst, dst)
        pushed.append(remote(src, there, weight_send.at[i], weight_recv.at[i], beside))
        loaded.append(pltpu.make_async_copy(src, here, load_sem.at[i]))
        loaded[-1].start()
    sent += [swap, raw]

    for i in range(2, 6):
        lay_out(i)
    gap = jnp.zeros((64, D), BF16)
    wqkv[320:HEAD_LANES, :] = gap
    wproj[0:64, :] = gap
    early[2].wait()
    own_count = count_all[d]
    for copy in loaded:
        copy.wait()
    for copy in pushed[:2]:
        copy.wait_recv()
    pieces = []
    for which in range(3):
        for core in range(2):
            pieces.append(bias_qkv[core, which : which + 1, :].astype(F32))
        if which == 0:
            pieces.append(jnp.zeros((1, 64), F32))
    wide_bias[...] = jnp.concatenate(pieces, axis=1)
    own_bias = fc1_own[...].astype(F32).reshape(1, 320)
    other_bias = fc1_other[...].astype(F32).reshape(1, 320)
    wide_fc1[...] = jnp.concatenate(
        [jnp.where(c == 0, own_bias, other_bias), jnp.where(c == 0, other_bias, own_bias)], axis=1
    )

    arrive(labels[1:])
    sent.append(labels[0])
    label_rows[...] = jnp.zeros(label_rows.shape, F32)
    for i in range(2 * CHIPS):
        label_rows[8 * i : 8 * i + TOKENS, :] = window_all[i].astype(F32)
    row, col = iotas((2 * GROUP, 16 * CHIPS))
    origin = jnp.where(row < GROUP, other, c)
    source = (row % GROUP // ROWS * 2 + origin) * 8 + row % ROWS // HALF
    spread_labels = matmul(one_hot(col == source), label_rows[...].astype(BF16))
    row, col = iotas((2 * GROUP, SLOTS))
    own_label = jnp.where(col == HALF * c + row % HALF, spread_labels, 0.0)
    own_label = jnp.sum(own_label, axis=1, keepdims=True).astype(jnp.int32)
    row, col = iotas((2 * GROUP, 128))
    marks = one_hot(col == own_label + 4 * (row % HALF))
    same = matmul_t(marks, marks)
    for copy in pushed[2:6]:
        copy.wait_recv()
    sent += pushed[:6]

    arrive(direct)
    arrive(forwarded)
    everything = jnp.concatenate([gathered(normed_all, k) for k in range(2)], axis=0).astype(BF16)
    qkv = (matmul_t(everything, wqkv[...]) + wide_bias[...]).astype(BF16)
    query, keys, values = (
        qkv[:, start : start + HEAD_LANES] for start in (0, HEAD_LANES, HEAD_LANES + 256)
    )
    row, lane = iotas((GROUP, HEAD_LANES))
    scale = 1.0 / (float(HEAD_DIM) ** 0.5)
    summing = []
    for k in range(2):
        part = query[GROUP * k : GROUP * (k + 1)]
        heads = []
        for j in range(HEADS):
            mask = (lane >= HEAD_DIM * j) & (lane < HEAD_DIM * (j + 1))
            heads.append(jnp.where(mask, part, 0.0).astype(BF16))
        scores = matmul_t(jnp.concatenate(heads, axis=0), keys) * scale
        inside = jnp.concatenate([same[GROUP * k : GROUP * (k + 1)] > 0.5] * HEADS, axis=0)
        weights = jnp.where(inside, jnp.exp(scores), 0.0)
        weights = weights / jnp.sum(weights, axis=1, keepdims=True)
        mixture = matmul(weights.astype(BF16), values)
        attended = jnp.zeros((GROUP, HEAD_LANES), F32)
        for j in range(HEADS):
            mask = (lane >= 64 + HEAD_DIM * j) & (lane < 64 + HEAD_DIM * (j + 1))
            attended = jnp.where(mask, mixture[GROUP * j : GROUP * (j + 1)], attended)
        mixed_part = matmul(attended.astype(BF16), wproj[...])
        part_out[k] = mixed_part.reshape(CHIPS, ROWS, D).astype(BF16)
        summing.append(scatter(part_out, part_in, 1, k))

    raw.wait_recv()
    kept[0] = raw_in[...].astype(F32)
    drain()
    moving = []
    for k in range(2):
        arrive(summing[k])
        mixed = (total(part_in, k) + vector(2) + kept[k]).astype(BF16).astype(F32)
        kept[k] = mixed + vector(5)
        normed2_all[k, y] = normalize(mixed, vector(3), vector(4)).astype(BF16)
        moving.append(spread(normed2_all, 2, k))

    for copy in pushed[6:]:
        copy.wait_recv()
    sent += pushed[6:]
    drain()
    summing = []
    for k in range(2):
        arrive(moving[k])
        activations = gathered(normed2_all, k).astype(BF16)
        lifted = matmul_t(activations, wfc1[...].reshape(640, D)) + wide_fc1[...]
        hidden = (lifted * jax.nn.sigmoid(1.702 * lifted)).astype(BF16)
        ffn_part = matmul(hidden, wfc2[...].reshape(640, D))
        ffn_out[k] = ffn_part.reshape(CHIPS, ROWS, D).astype(BF16)
        summing.append(scatter(ffn_out, ffn_in, 3, k))

    drain()
    row, col = iotas((ROWS, D))
    live = HALF * c + row % HALF < own_count
    arrive(summing[0])
    done_out[...] = jnp.where(live, total(ffn_in, 0) + kept[0], 0.0).astype(BF16)
    back = remote(done_out, done_in, swap_send.at[2], swap_recv.at[2], beside)
    arrive(summing[1])
    mine = jnp.where(live, total(ffn_in, 1) + kept[1], 0.0)
    arrive([back])
    theirs = done_in[...].astype(F32)
    low, high = jnp.where(c == 0, mine, theirs), jnp.where(c == 0, theirs, mine)
    for i in range(TOKENS):
        rows = [part[HALF * i : HALF * (i + 1)] for part in (low, high)]
        out[i] = jnp.concatenate(rows, axis=0).astype(BF16)
    drain()


def on_device(
    tiles,
    window_ids,
    counts,
    ln_gain,
    ln_bias,
    qkv_weight,
    qkv_bias,
    proj_weight,
    proj_bias,
    mlp_gain,
    mlp_bias,
    fc1_weight,
    fc1_bias,
    fc2_weight,
    fc2_bias,
):
    operands = (
        counts,
        jnp.transpose(window_ids),
        jnp.transpose(tiles, (1, 0, 2)),
        ln_gain,
        ln_bias,
        jnp.swapaxes(qkv_weight, 1, 2),
        qkv_bias,
        proj_weight,
        proj_bias,
        mlp_gain,
        mlp_bias,
        jnp.transpose(fc1_weight),
        fc1_bias,
        fc2_weight,
        fc2_bias,
    )
    encoded = pl.pallas_call(
        encode,
        out_shape=pltpu.VMEM((TOKENS, SLOTS, D), BF16),
        in_specs=[pl.BlockSpec(memory_space=pltpu.HBM)] * len(operands),
        out_specs=pl.BlockSpec(memory_space=pltpu.VMEM),
        scratch_shapes=[
            pltpu.SMEM((64,), jnp.int32),
            pltpu.VMEM((2 * CHIPS, TOKENS, SLOTS), jnp.int32),
            pltpu.VMEM((16 * CHIPS, SLOTS), F32),
            [pltpu.VMEM((D,), BF16)] * 6,
            pltpu.VMEM((2, 3, 160), BF16),
            pltpu.VMEM((320,), BF16),
            pltpu.VMEM((320,), BF16),
            pltpu.VMEM((8, D), F32),
            pltpu.VMEM((1, 1024), F32),
            pltpu.VMEM((1, 640), F32),
            pltpu.VMEM((1024, D), BF16),
            pltpu.VMEM((HEAD_LANES, D), BF16),
            pltpu.VMEM((2, 320, D), BF16),
            pltpu.VMEM((2, 320, D), BF16),
            pltpu.VMEM((TOKENS, SLOTS, D), BF16),
            pltpu.VMEM((ROWS, D), BF16),
            pltpu.VMEM((ROWS, D), BF16),
            pltpu.VMEM((ROWS, D), BF16),
            pltpu.VMEM((2, ROWS, D), F32),
            pltpu.VMEM((2, CHIPS, ROWS, D), BF16),
            pltpu.VMEM((2, CHIPS, ROWS, D), BF16),
            pltpu.VMEM((2, CHIPS, ROWS, D), BF16),
            pltpu.VMEM((2, CHIPS, ROWS, D), BF16),
            pltpu.VMEM((2, CHIPS, ROWS, D), BF16),
            pltpu.VMEM((2, CHIPS, ROWS, D), BF16),
            pltpu.VMEM((ROWS, D), BF16),
            pltpu.VMEM((ROWS, D), BF16),
            pltpu.SemaphoreType.DMA((3,)),
            pltpu.SemaphoreType.DMA((6,)),
            pltpu.SemaphoreType.DMA((8,)),
            pltpu.SemaphoreType.DMA((8,)),
            pltpu.SemaphoreType.DMA((8,)),
            pltpu.SemaphoreType.DMA((7,)),
            pltpu.SemaphoreType.DMA((7,)),
            pltpu.SemaphoreType.DMA((3,)),
            pltpu.SemaphoreType.DMA((3,)),
            pltpu.SemaphoreType.DMA((4, 2, 3)),
            pltpu.SemaphoreType.DMA((4, 2, 3)),
        ],
        compiler_params=pltpu.CompilerParams(
            collective_id=0, has_side_effects=True, vmem_limit_bytes=48 * 2**20
        ),
        name="encode",
    )(*(pltpu.with_memory_space_constraint(operand, pltpu.HBM) for operand in operands))
    return jnp.transpose(encoded, (1, 0, 2))


def solution(mesh):
    placed = (
        P("dp", "tensor", None),
        P("dp", "tensor"),
        P(),
        P(),
        P(),
        P(None, None, "tensor"),
        P(None, "tensor"),
        P("tensor", None),
        P(),
        P(),
        P(),
        P(None, "tensor"),
        P("tensor"),
        P("tensor", None),
        P(),
    )
    return jax.shard_map(
        on_device, mesh=mesh, in_specs=placed, out_specs=P("dp", "tensor", None), check_vma=False
    )
```

time: 41.6 us -> 38.5 us (0.925)
  Pallas kernels: 40.8 us -> 37.7 us
    pallas_call x1, Pallas kernels: 40.8 us -> 37.7 us  [on_device(): pl.pallas_call(encode, out_shape=pltpu.VMEM((TOKENS, SLOTS, D), BF16), in...]
where the time goes in v5:
time: 38.5 us; the launch traced here: 38.4 us
  Pallas kernels  37.7 us (98%)
  local copies, waits for them, and re-layouts  0.65 us (2%)
    pallas_call x1, Pallas kernels, on_device(): pl.pallas_call(encode, out_shape=pltpu.VMEM((TOKENS, SLOTS, D), BF16), in...  37.7 us

profile of v5, /device:TPU:1, one launch (start us, length us, event | category | flops | bytes accessed | tf_op | source)
XLA Modules:
  0.0 38.4 jit_solution(10686531699128772099)
XLA Ops:
  0.0 37.7 %encode.1 = bf16[3,16,1280]{2,1,0:T(8,128)(2,1)S(1)} custom-call(s32[64]{0:T(128)} %counts.1, s32[3,16]{1,0:T(4,128)} %bitcast.9, bf16[3,16,1280]{2,1,0:T(8,128)(2,1)} %bitcast.8, bf16[1280]{0:T(1024)(128)(2,1)} %ln_gain.1, bf16[1280]{0:T(1024)(128)(2,1)} %ln_bias.1, bf16[3,160,1280]{2,1,0:T(8,128)(2,1)} %bitcast.6, bf16[3,160]{1,0:T(4,128)(2,1)} %qkv_bias.1, ...), custom_call_target="tpu_custom_call" | custom-call | tf_op jit(solution)/shard_map/encode/pallas_call | solution.py:387
  37.7 0.7 %copy.17 = bf16[16,3,1280]{2,0,1:T(8,128)(2,1)} copy(bf16[16,3,1280]{2,0,1:T(8,128)(2,1)S(1)} %bitcast.5) | data formatting | bytes 245760

commit v6 on v5

--- a/solution.py
+++ b/solution.py
@@ -76,6 +76,8 @@
     wproj,
     wfc1,
     wfc2,
+    wqkv_t,
+    wfc1_t,
     tile_rows,
     swap_out,
     raw_out,
@@ -203,24 +205,24 @@
             out_sum = out_sum + buffer[k, i].astype(F32)
         return out_sum
 
-    swap = remote(swap_out, normed_all.at[0, y], swap_send.at[0], swap_recv.at[0], beside)
-    direct = spread(normed_all, 0, 1)
-
     def label(i, of, peer):
         return remote(
             window_all.at[of], window_all.at[of], label_send.at[i], label_recv.at[i], peer
         )
 
     early[1].wait()
-    labels = [label(i, t, peer) for i, peer in enumerate([beside] + around)]
+    labels = [label(0, t, beside)]
+    swap = remote(swap_out, normed_all.at[0, y], swap_send.at[0], swap_recv.at[0], beside)
+    labels += [label(1 + i, t, peer) for i, peer in enumerate(around)]
+    direct = spread(normed_all, 0, 1)
     mine, theirs = halves(features)
     kept[1] = mine
     raw_out[...] = theirs.astype(BF16)
     raw = remote(raw_out, raw_in, swap_send.at[1], swap_recv.at[1], beside)
+    labels[0].wait_recv()
+    labels += [label(4 + i, beside[1], peer) for i, peer in enumerate(around)]
     swap.wait_recv()
     forwarded = spread(normed_all, 0, 0)
-    labels[0].wait_recv()
-    labels += [label(4 + i, beside[1], peer) for i, peer in enumerate(around)]
 
     mine_at = pl.multiple_of(c * 160, 16)
     pairs = [(qkv_bias, bias_qkv.at[c]), (fc1_bias, None)]
@@ -260,37 +262,39 @@
         [jnp.where(c == 0, own_bias, other_bias), jnp.where(c == 0, other_bias, own_bias)], axis=1
     )
 
-    arrive(labels[1:])
-    sent.append(labels[0])
-    label_rows[...] = jnp.zeros(label_rows.shape, F32)
-    for i in range(2 * CHIPS):
-        label_rows[8 * i : 8 * i + TOKENS, :] = window_all[i].astype(F32)
-    row, col = iotas((2 * GROUP, 16 * CHIPS))
-    origin = jnp.where(row < GROUP, other, c)
-    source = (row % GROUP // ROWS * 2 + origin) * 8 + row % ROWS // HALF
-    spread_labels = matmul(one_hot(col == source), label_rows[...].astype(BF16))
-    row, col = iotas((2 * GROUP, SLOTS))
-    own_label = jnp.where(col == HALF * c + row % HALF, spread_labels, 0.0)
-    own_label = jnp.sum(own_label, axis=1, keepdims=True).astype(jnp.int32)
-    row, col = iotas((2 * GROUP, 128))
-    marks = one_hot(col == own_label + 4 * (row % HALF))
-    same = matmul_t(marks, marks)
     for copy in pushed[2:6]:
         copy.wait_recv()
     sent += pushed[:6]
-
-    arrive(direct)
-    arrive(forwarded)
-    everything = jnp.concatenate([gathered(normed_all, k) for k in range(2)], axis=0).astype(BF16)
-    qkv = (matmul_t(everything, wqkv[...]) + wide_bias[...]).astype(BF16)
-    query, keys, values = (
-        qkv[:, start : start + HEAD_LANES] for start in (0, HEAD_LANES, HEAD_LANES + 256)
-    )
+    wqkv_t[...] = wqkv[...].T
+
+    qkv = [None, None]
+    for k, copies in ((1, direct), (0, forwarded)):
+        arrive(copies)
+        rows = gathered(normed_all, k).astype(BF16)
+        qkv[k] = (matmul(rows, wqkv_t[...]) + wide_bias[...]).astype(BF16)
+        if k == 1:
+            arrive(labels[1:])
+            sent.append(labels[0])
+            label_rows[...] = jnp.zeros(label_rows.shape, F32)
+            for i in range(2 * CHIPS):
+                label_rows[8 * i : 8 * i + TOKENS, :] = window_all[i].astype(F32)
+            row, col = iotas((2 * GROUP, 16 * CHIPS))
+            origin = jnp.where(row < GROUP, other, c)
+            source = (row % GROUP // ROWS * 2 + origin) * 8 + row % ROWS // HALF
+            spread_labels = matmul(one_hot(col == source), label_rows[...].astype(BF16))
+            row, col = iotas((2 * GROUP, SLOTS))
+            own_label = jnp.where(col == HALF * c + row % HALF, spread_labels, 0.0)
+            own_label = jnp.sum(own_label, axis=1, keepdims=True).astype(jnp.int32)
+            row, col = iotas((2 * GROUP, 128))
+            marks = one_hot(col == own_label + 4 * (row % HALF))
+            same = matmul_t(marks, marks)
+    keys = jnp.concatenate([part[:, HEAD_LANES : 2 * HEAD_LANES] for part in qkv], axis=0)
+    values = jnp.concatenate([part[:, HEAD_LANES + 256 :] for part in qkv], axis=0)
     row, lane = iotas((GROUP, HEAD_LANES))
     scale = 1.0 / (float(HEAD_DIM) ** 0.5)
     summing = []
     for k in range(2):
-        part = query[GROUP * k : GROUP * (k + 1)]
+        part = qkv[k][:, :HEAD_LANES]
         heads = []
         for j in range(HEADS):
             mask = (lane >= HEAD_DIM * j) & (lane < HEAD_DIM * (j + 1))
@@ -308,6 +312,10 @@
         part_out[k] = mixed_part.reshape(CHIPS, ROWS, D).astype(BF16)
         summing.append(scatter(part_out, part_in, 1, k))
 
+    for copy in pushed[6:]:
+        copy.wait_recv()
+    sent += pushed[6:]
+    wfc1_t[...] = wfc1[...].reshape(640, D).T
     raw.wait_recv()
     kept[0] = raw_in[...].astype(F32)
     drain()
@@ -319,15 +327,12 @@
         normed2_all[k, y] = normalize(mixed, vector(3), vector(4)).astype(BF16)
         moving.append(spread(normed2_all, 2, k))
 
-    for copy in pushed[6:]:
-        copy.wait_recv()
-    sent += pushed[6:]
     drain()
     summing = []
     for k in range(2):
         arrive(moving[k])
         activations = gathered(normed2_all, k).astype(BF16)
-        lifted = matmul_t(activations, wfc1[...].reshape(640, D)) + wide_fc1[...]
+        lifted = matmul(activations, wfc1_t[...]) + wide_fc1[...]
         hidden = (lifted * jax.nn.sigmoid(1.702 * lifted)).astype(BF16)
         ffn_part = matmul(hidden, wfc2[...].reshape(640, D))
         ffn_out[k] = ffn_part.reshape(CHIPS, ROWS, D).astype(BF16)
@@ -404,6 +409,8 @@
             pltpu.VMEM((HEAD_LANES, D), BF16),
             pltpu.VMEM((2, 320, D), BF16),
             pltpu.VMEM((2, 320, D), BF16),
+            pltpu.VMEM((D, 1024), BF16),
+            pltpu.VMEM((D, 640), BF16),
             pltpu.VMEM((TOKENS, SLOTS, D), BF16),
             pltpu.VMEM((ROWS, D), BF16),
             pltpu.VMEM((ROWS, D), BF16),

time: 38.5 us -> 37.3 us (0.969)
  Pallas kernels: 37.7 us -> 36.5 us
    pallas_call x1, Pallas kernels: 37.7 us -> 36.5 us  [on_device(): pl.pallas_call(encode, out_shape=pltpu.VMEM((TOKENS, SLOTS, D), BF16), in...]
where the time goes in v6:
time: 37.3 us; the launch traced here: 37.1 us
  Pallas kernels  36.5 us (98%)
  local copies, waits for them, and re-layouts  0.65 us (2%)
    pallas_call x1, Pallas kernels, on_device(): pl.pallas_call(encode, out_shape=pltpu.VMEM((TOKENS, SLOTS, D), BF16), in...  36.5 us

profile of v6, /device:TPU:1, one launch (start us, length us, event | category | flops | bytes accessed | tf_op | source)
XLA Modules:
  0.0 37.1 jit_solution(15120306320427710516)
XLA Ops:
  0.0 36.5 %encode.1 = bf16[3,16,1280]{2,1,0:T(8,128)(2,1)S(1)} custom-call(s32[64]{0:T(128)} %counts.1, s32[3,16]{1,0:T(4,128)} %bitcast.9, bf16[3,16,1280]{2,1,0:T(8,128)(2,1)} %bitcast.8, bf16[1280]{0:T(1024)(128)(2,1)} %ln_gain.1, bf16[1280]{0:T(1024)(128)(2,1)} %ln_bias.1, bf16[3,160,1280]{2,1,0:T(8,128)(2,1)} %bitcast.6, bf16[3,160]{1,0:T(4,128)(2,1)} %qkv_bias.1, ...), custom_call_target="tpu_custom_call" | custom-call | tf_op jit(solution)/shard_map/encode/pallas_call | solution.py:392
  36.5 0.7 %copy.17 = bf16[16,3,1280]{2,0,1:T(8,128)(2,1)} copy(bf16[16,3,1280]{2,0,1:T(8,128)(2,1)S(1)} %bitcast.5) | data formatting | bytes 245760

commit v7 on v6

--- a/solution.py
+++ b/solution.py
@@ -290,24 +290,27 @@
             same = matmul_t(marks, marks)
     keys = jnp.concatenate([part[:, HEAD_LANES : 2 * HEAD_LANES] for part in qkv], axis=0)
     values = jnp.concatenate([part[:, HEAD_LANES + 256 :] for part in qkv], axis=0)
-    row, lane = iotas((GROUP, HEAD_LANES))
+    row, lane = iotas((1, HEAD_LANES))
     scale = 1.0 / (float(HEAD_DIM) ** 0.5)
+    spans = [(lane >= HEAD_DIM * j) & (lane < HEAD_DIM * (j + 1)) for j in range(HEADS)]
+    outs = [
+        (lane >= 64 + HEAD_DIM * j) & (lane < 64 + HEAD_DIM * (j + 1)) for j in range(HEADS)
+    ]
+    spans = [one_hot(span) for span in spans]
     summing = []
     for k in range(2):
         part = qkv[k][:, :HEAD_LANES]
-        heads = []
+        scores = matmul_t(jnp.concatenate([part * span for span in spans], axis=0), keys)
+        inside = same[GROUP * k : GROUP * (k + 1)] > 0.5
+        weights = []
         for j in range(HEADS):
-            mask = (lane >= HEAD_DIM * j) & (lane < HEAD_DIM * (j + 1))
-            heads.append(jnp.where(mask, part, 0.0).astype(BF16))
-        scores = matmul_t(jnp.concatenate(heads, axis=0), keys) * scale
-        inside = jnp.concatenate([same[GROUP * k : GROUP * (k + 1)] > 0.5] * HEADS, axis=0)
-        weights = jnp.where(inside, jnp.exp(scores), 0.0)
-        weights = weights / jnp.sum(weights, axis=1, keepdims=True)
-        mixture = matmul(weights.astype(BF16), values)
+            grown = jnp.exp(scores[GROUP * j : GROUP * (j + 1)] * scale)
+            grown = jnp.where(inside, grown, 0.0)
+            weights.append((grown / jnp.sum(grown, axis=1, keepdims=True)).astype(BF16))
+        mixture = matmul(jnp.concatenate(weights, axis=0), values)
         attended = jnp.zeros((GROUP, HEAD_LANES), F32)
         for j in range(HEADS):
-            mask = (lane >= 64 + HEAD_DIM * j) & (lane < 64 + HEAD_DIM * (j + 1))
-            attended = jnp.where(mask, mixture[GROUP * j : GROUP * (j + 1)], attended)
+            attended = jnp.where(outs[j], mixture[GROUP * j : GROUP * (j + 1)], attended)
         mixed_part = matmul(attended.astype(BF16), wproj[...])
         part_out[k] = mixed_part.reshape(CHIPS, ROWS, D).astype(BF16)
         summing.append(scatter(part_out, part_in, 1, k))

time: 37.3 us -> 37.3 us (level)
  no operation moved by 1% of the time
where the time goes in v7:
time: 37.3 us; the launch traced here: 37.1 us
  Pallas kernels  36.5 us (98%)
  local copies, waits for them, and re-layouts  0.65 us (2%)
    pallas_call x1, Pallas kernels, on_device(): pl.pallas_call(encode, out_shape=pltpu.VMEM((TOKENS, SLOTS, D), BF16), in...  36.5 us

profile of v7, /device:TPU:1, one launch (start us, length us, event | category | flops | bytes accessed | tf_op | source)
XLA Modules:
  0.0 37.1 jit_solution(5963994633453920200)
XLA Ops:
  0.0 36.5 %encode.1 = bf16[3,16,1280]{2,1,0:T(8,128)(2,1)S(1)} custom-call(s32[64]{0:T(128)} %counts.1, s32[3,16]{1,0:T(4,128)} %bitcast.9, bf16[3,16,1280]{2,1,0:T(8,128)(2,1)} %bitcast.8, bf16[1280]{0:T(1024)(128)(2,1)} %ln_gain.1, bf16[1280]{0:T(1024)(128)(2,1)} %ln_bias.1, bf16[3,160,1280]{2,1,0:T(8,128)(2,1)} %bitcast.6, bf16[3,160]{1,0:T(4,128)(2,1)} %qkv_bias.1, ...), custom_call_target="tpu_custom_call" | custom-call | tf_op jit(solution)/shard_map/encode/pallas_call | solution.py:395
  36.5 0.7 %copy.17 = bf16[16,3,1280]{2,0,1:T(8,128)(2,1)} copy(bf16[16,3,1280]{2,0,1:T(8,128)(2,1)S(1)} %bitcast.5) | data formatting | bytes 245760

commit v8 on v7

--- a/solution.py
+++ b/solution.py
@@ -314,11 +314,12 @@
         mixed_part = matmul(attended.astype(BF16), wproj[...])
         part_out[k] = mixed_part.reshape(CHIPS, ROWS, D).astype(BF16)
         summing.append(scatter(part_out, part_in, 1, k))
-
-    for copy in pushed[6:]:
-        copy.wait_recv()
-    sent += pushed[6:]
-    wfc1_t[...] = wfc1[...].reshape(640, D).T
+        if k == 0:
+            for copy in pushed[6:]:
+                copy.wait_recv()
+            sent += pushed[6:]
+            wfc1_t[...] = wfc1[...].reshape(640, D).T
+
     raw.wait_recv()
     kept[0] = raw_in[...].astype(F32)
     drain()
@@ -349,6 +350,7 @@
     back = remote(done_out, done_in, swap_send.at[2], swap_recv.at[2], beside)
     arrive(summing[1])
     mine = jnp.where(live, total(ffn_in, 1) + kept[1], 0.0)
+    drain()
     arrive([back])
     theirs = done_in[...].astype(F32)
     low, high = jnp.where(c == 0, mine, theirs), jnp.where(c == 0, theirs, mine)

time: 37.3 us -> 37 us (level)
  no operation moved by 1% of the time
where the time goes in v8:
time: 37 us; the launch traced here: 36.9 us
  Pallas kernels  36.2 us (98%)
  local copies, waits for them, and re-layouts  0.65 us (2%)
    pallas_call x1, Pallas kernels, on_device(): pl.pallas_call(encode, out_shape=pltpu.VMEM((TOKENS, SLOTS, D), BF16), in...  36.2 us

profile of v8, /device:TPU:1, one launch (start us, length us, event | category | flops | bytes accessed | tf_op | source)
XLA Modules:
  0.0 36.9 jit_solution(1260387966283952404)
XLA Ops:
  0.0 36.2 %encode.1 = bf16[3,16,1280]{2,1,0:T(8,128)(2,1)S(1)} custom-call(s32[64]{0:T(128)} %counts.1, s32[3,16]{1,0:T(4,128)} %bitcast.9, bf16[3,16,1280]{2,1,0:T(8,128)(2,1)} %bitcast.8, bf16[1280]{0:T(1024)(128)(2,1)} %ln_gain.1, bf16[1280]{0:T(1024)(128)(2,1)} %ln_bias.1, bf16[3,160,1280]{2,1,0:T(8,128)(2,1)} %bitcast.6, bf16[3,160]{1,0:T(4,128)(2,1)} %qkv_bias.1, ...), custom_call_target="tpu_custom_call" | custom-call | tf_op jit(solution)/shard_map/encode/pallas_call | solution.py:397
  36.2 0.7 %copy.17 = bf16[16,3,1280]{2,0,1:T(8,128)(2,1)} copy(bf16[16,3,1280]{2,0,1:T(8,128)(2,1)S(1)} %bitcast.5) | data formatting | bytes 245760

commit v9 on v8

--- a/solution.py
+++ b/solution.py
@@ -215,15 +215,6 @@
     swap = remote(swap_out, normed_all.at[0, y], swap_send.at[0], swap_recv.at[0], beside)
     labels += [label(1 + i, t, peer) for i, peer in enumerate(around)]
     direct = spread(normed_all, 0, 1)
-    mine, theirs = halves(features)
-    kept[1] = mine
-    raw_out[...] = theirs.astype(BF16)
-    raw = remote(raw_out, raw_in, swap_send.at[1], swap_recv.at[1], beside)
-    labels[0].wait_recv()
-    labels += [label(4 + i, beside[1], peer) for i, peer in enumerate(around)]
-    swap.wait_recv()
-    forwarded = spread(normed_all, 0, 0)
-
     mine_at = pl.multiple_of(c * 160, 16)
     pairs = [(qkv_bias, bias_qkv.at[c]), (fc1_bias, None)]
     for which, start in enumerate((0, HEAD_LANES, HEAD_LANES + 320)):
@@ -231,11 +222,26 @@
     pairs.append((proj_weight, wproj.at[pl.ds(64 + mine_at, 160)]))
     pairs += [(fc1_weight, wfc1.at[c]), (fc2_weight, wfc2.at[c])]
     pushed, loaded = [], []
-    for i, (src, dst) in enumerate(pairs):
+    def share(i):
+        src, dst = pairs[i]
         there, here = (fc1_other, fc1_own) if dst is None else (dst, dst)
         pushed.append(remote(src, there, weight_send.at[i], weight_recv.at[i], beside))
         loaded.append(pltpu.make_async_copy(src, here, load_sem.at[i]))
         loaded[-1].start()
+
+    for i in range(6):
+        share(i)
+    mine, theirs = halves(features)
+    kept[1] = mine
+    labels[0].wait_recv()
+    labels += [label(4 + i, beside[1], peer) for i, peer in enumerate(around)]
+    swap.wait_recv()
+    forwarded = spread(normed_all, 0, 0)
+    raw_out[...] = theirs.astype(BF16)
+    raw = remote(raw_out, raw_in, swap_send.at[1], swap_recv.at[1], beside)
+
+    for i in range(6, len(pairs)):
+        share(i)
     sent += [swap, raw]
 
     for i in range(2, 6):

time: 37 us -> 37.1 us (level)
  no operation moved by 1% of the time
where the time goes in v9:
time: 37.1 us; the launch traced here: 37 us
  Pallas kernels  36.3 us (98%)
  local copies, waits for them, and re-layouts  0.65 us (2%)
    pallas_call x1, Pallas kernels, on_device(): pl.pallas_call(encode, out_shape=pltpu.VMEM((TOKENS, SLOTS, D), BF16), in...  36.3 us

profile of v9, /device:TPU:1, one launch (start us, length us, event | category | flops | bytes accessed | tf_op | source)
XLA Modules:
  0.0 37.0 jit_solution(1280341583332492293)
XLA Ops:
  0.0 36.3 %encode.1 = bf16[3,16,1280]{2,1,0:T(8,128)(2,1)S(1)} custom-call(s32[64]{0:T(128)} %counts.1, s32[3,16]{1,0:T(4,128)} %bitcast.9, bf16[3,16,1280]{2,1,0:T(8,128)(2,1)} %bitcast.8, bf16[1280]{0:T(1024)(128)(2,1)} %ln_gain.1, bf16[1280]{0:T(1024)(128)(2,1)} %ln_bias.1, bf16[3,160,1280]{2,1,0:T(8,128)(2,1)} %bitcast.6, bf16[3,160]{1,0:T(4,128)(2,1)} %qkv_bias.1, ...), custom_call_target="tpu_custom_call" | custom-call | tf_op jit(solution)/shard_map/encode/pallas_call | solution.py:403
  36.3 0.7 %copy.17 = bf16[16,3,1280]{2,0,1:T(8,128)(2,1)} copy(bf16[16,3,1280]{2,0,1:T(8,128)(2,1)S(1)} %bitcast.5) | data formatting | bytes 245760
